TPU v7x, 32 devices: a whole 2x2x4 slice. The times are simulated.
32 devices in a mesh: member: 8 (over z, x), wave: 4 (over y, core).
Axes of the slice: x: 2, y: 2, z: 4, core: 2. Of those that a mesh axis runs over, the one named last changes fastest.
Arguments:
- state: float32 [8, 32, 32, 640], P('member', 'wave'), may hold values from -6 to 6
- legendre: bfloat16 [32, 640, 640], P('wave'), may hold values from -0.25 to 0.25
- lat_weights: float32 [640], replicated, may hold values from 0.5 to 2
- region: int32 [4], replicated, may hold values from 0 to 2560, as said below
- sources: int32 [8], replicated, may hold values from 0 to 7, as said below
Outputs:
- new_states: float32 [8, 32, 32, 640], P('member', 'wave')
- scores: float32 [8], P('member')
Inputs may be any that keep to these rules, and one draw needn't show every extreme that they name: region[0] < region[1] bound the latitudes and region[2] < region[3] the longitudes of the region; each band covers at least half of its grid dimension; the longitude band ends at the last longitude, region[3] = 2560. `sources`: some member is the source of at least 2 slots.
All inputs are finite; a program needn't handle non-finite values.
Results may differ from a plain program's by a relative error of at most 0.0059.
Values may be sent and summed in bfloat16 or wider, within the bound.
A program may use at most 128 MiB of HBM per device.

v0:
```python
import jax
import jax.numpy as jnp
from jax import lax
from jax.sharding import PartitionSpec as P

NLON = 2560


advect_rate = 2.0


def fourier_table(waves_total, points):
    wave_index = lax.broadcasted_iota(jnp.int32, (waves_total, points), 0)
    column_index = lax.broadcasted_iota(jnp.int32, (waves_total, points), 1)
    angles = (wave_index * column_index % points).astype(jnp.float32) * (2.0 * jnp.pi / points)
    return jnp.stack([jnp.cos(angles), -jnp.sin(angles)], axis=1).astype(jnp.bfloat16)


def on_device(state, legendre, lat_weights, region, sources):
    wave_count = lax.axis_size("wave")
    waves_local = legendre.shape[0]
    waves_total = waves_local * wave_count
    degrees = legendre.shape[1]
    latitudes = legendre.shape[2]
    lat_rows = latitudes // wave_count
    state_rows = state.shape[2]
    level_count = state_rows // 4
    fourier = fourier_table(waves_total, NLON)
    spectral = state[0]
    fourier_coef = jnp.einsum(
        "mrn,mnl->mrl", spectral.astype(jnp.bfloat16), legendre, preferred_element_type=jnp.float32
    )
    fourier_coef = fourier_coef.astype(jnp.bfloat16).reshape(
        waves_local, 2, 2 * level_count, latitudes
    )
    synthesis_scale = (2.0 * waves_total) ** (-0.5)
    gridded = synthesis_scale * jnp.einsum(
        "mckl,mcx->klx",
        lax.all_to_all(fourier_coef, "wave", split_axis=3, concat_axis=0, tiled=True),
        fourier,
        preferred_element_type=jnp.float32,
    )
    lat_start = lax.axis_index("wave") * lat_rows
    local_weights = lax.dynamic_slice_in_dim(lat_weights, lat_start, lat_rows)
    wind_grid = gridded[:level_count]
    temper_grid = gridded[level_count:]
    fluxes = (
        jnp.concatenate([0.5 * wind_grid * wind_grid, wind_grid * temper_grid], axis=0)
        * local_weights[None, :, None]
    )
    fluxes = fluxes.astype(jnp.bfloat16)
    lat_index = lat_start + lax.broadcasted_iota(jnp.int32, (lat_rows, 1), 0)
    lon_index = lax.broadcasted_iota(jnp.int32, (1, NLON), 1)
    in_region = (
        (lat_index >= region[0])
        & (lat_index < region[1])
        & (lon_index >= region[2])
        & (lon_index < region[3])
    )
    lowest = temper_grid[level_count - 1]
    region_part = jnp.sum(jnp.where(in_region, local_weights[:, None] * lowest * lowest, 0.0))
    region_total = lax.psum(region_part, "wave")
    every_lat = lax.broadcasted_iota(jnp.int32, (latitudes,), 0)
    lat_inside = (every_lat >= region[0]) & (every_lat < region[1])
    region_weight = jnp.sum(jnp.where(lat_inside, lat_weights, 0.0)) * (
        region[3] - region[2]
    ).astype(jnp.float32)
    scores = (region_total / region_weight).reshape(1)
    analysis_scale = NLON ** (-0.5)
    flux_coef = analysis_scale * jnp.einsum(
        "klx,mcx->mckl", fluxes, fourier, preferred_element_type=jnp.float32
    )
    flux_coef = flux_coef.astype(jnp.bfloat16)
    tendency = jnp.einsum(
        "mckl,mnl->mckn",
        lax.all_to_all(flux_coef, "wave", split_axis=0, concat_axis=3, tiled=True),
        legendre,
        preferred_element_type=jnp.float32,
    )
    wave_ids = lax.axis_index("wave") * waves_local + lax.broadcasted_iota(
        jnp.int32, (waves_local, 1, 1), 0
    )
    advection = advect_rate * wave_ids.astype(jnp.float32) / waves_total
    degree_ids = lax.broadcasted_iota(jnp.int32, (1, 1, degrees), 2).astype(jnp.float32)
    damping = 1.0 + ((degree_ids + 1.0) / degrees) ** 2
    spectral_split = spectral.reshape(waves_local, 2, 2 * level_count, degrees)
    real_part = (spectral_split[:, 0] + advection * tendency[:, 1]) / damping
    imag_part = (spectral_split[:, 1] - advection * tendency[:, 0]) / damping
    stepped = jnp.stack([real_part, imag_part], axis=1).reshape(1, waves_local, state_rows, degrees)
    source_member = sources[lax.axis_index("member")]
    shards = lax.all_gather(stepped, "member", axis=0, tiled=True)
    owners = lax.broadcasted_iota(jnp.int32, (shards.shape[0], 1, 1, 1), 0)
    cloned = jnp.sum(jnp.where(owners == source_member, shards, 0.0), axis=0, keepdims=True)
    return (cloned, scores)


def solution(mesh):
    in_specs = (P("member", "wave", None, None), P("wave", None, None), P(), P(), P())
    out_specs = (P("member", "wave", None, None), P("member"))
    return jax.shard_map(
        on_device, mesh=mesh, in_specs=in_specs, out_specs=out_specs, check_vma=False
    )
```

profile of v0, /device:TPU:0, one launch (start us, length us, event | category | flops | bytes accessed | tf_op | source)
XLA Modules:
  0.0 186.2 jit_solution(8054573911200346946)
XLA Ops:
  7.2 0.0 copy-start.3
  7.2 4.2 %convolution_convert_fusion = bf16[8,32,640]{2,1,0:T(8,128)(2,1)S(1)} fusion(bf16[8,640,640]{2,1,0:T(8,128)(2,1)} %param.6, f32[1,8,32,640]{3,2,1,0:T(8,128)} %param.5), kind=kOutput, calls=%fused_computation.16 | convolution fusion | flops 210042880 | bytes 7536640 | tf_op jit(solution)/shard_map/mrn,mnl->mrl/dot_general | solution.py:30
  11.4 3.3 %copy.9 = bf16[8,2,16,640]{2,1,0,3:T(2,128)(2,1)S(1)} copy(bf16[8,2,16,640]{3,2,1,0:T(8,128)(2,1)S(1)} %bitcast.57) | data formatting | bytes 655360 | tf_op jit(solution)/shard_map/reshape | solution.py:33
  14.7 3.4 %reshape.118 = bf16[4,2,20480]{2,1,0:T(2,128)(2,1)} reshape(bf16[640,8,2,16]{3,2,1,0:T(2,128)(2,1)S(1)} %bitcast.53) | data formatting | bytes 655360
  18.0 4.2 %all-to-all-start = ((bf16[4,2,20480]{2,1,0:T(2,128)(2,1)}), bf16[4,2,20480]{2,1,0:T(2,128)(2,1)S(1)}, u32[]{:S(2)}, u32[]{:S(2)}) async-start(bf16[4,2,20480]{2,1,0:T(2,128)(2,1)} %reshape.118), calls=%async_computation | async-start | bytes 655360 | tf_op jit(solution)/shard_map/all_to_all | solution.py:39
  22.3 0.0 copy-done.3
  22.3 0.1 dynamic_slice.7
  22.4 1.4 negate_convert_fusion
  23.7 5.3 %all-to-all-done = bf16[4,2,20480]{2,1,0:T(2,128)(2,1)S(1)} async-done(((bf16[4,2,20480]{2,1,0:T(2,128)(2,1)}), bf16[4,2,20480]{2,1,0:T(2,128)(2,1)S(1)}, u32[]{:S(2)}, u32[]{:S(2)}) %all-to-all-start) | async-done | bytes 327712 | tf_op jit(solution)/shard_map/all_to_all | solution.py:39
  29.0 1.9 reshape.119
  30.9 4.7 %copy.10 = bf16[8,2,16,4,160]{4,0,3,1,2:T(8,128)(2,1)S(1)} copy(bf16[8,2,16,4,160]{2,1,0,4,3:T(2,128)(2,1)S(1)} %bitcast.54) | data formatting | bytes 655360 | tf_op jit(solution)/shard_map/all_to_all | solution.py:39
  35.6 3.6 %bitcast_multiply_fusion = f32[16,160,2560]{2,1,0:T(8,128)S(1)} fusion(bf16[8,2,16,4,160]{4,0,3,1,2:T(8,128)(2,1)S(1)} %copy.10, bf16[32,1,2560]{2,0,1:T(8,128)(2,1)S(1)} %get-tuple-element.10, bf16[32,1,2560]{2,0,1:T(8,128)(2,1)S(1)} %get-tuple-element.11), kind=kOutput, calls=%fused_computation.2 | convolution fusion | flops 845578240 | bytes 26869760 | tf_op jit(solution)/shard_map/mckl,mcx->klx/dot_general | solution.py:37
  39.2 0.0 copy-start
  39.2 10.1 %multiply_multiply_fusion = (f32[8,160,2560]{2,1,0:T(8,128)}, f32[8,160,2560]{2,1,0:T(8,128)}) fusion(f32[16,160,2560]{2,1,0:T(8,128)S(1)} %bitcast_multiply_fusion), kind=kLoop, calls=%fused_computation.3 | loop fusion | flops 9830400 | bytes 52428800 | tf_op jit(solution)/shard_map/mul | solution.py:48
  49.3 6.4 %copy-done = f32[16,160,2560]{2,1,0:T(8,128)} copy-done((f32[16,160,2560]{2,1,0:T(8,128)}, f32[16,160,2560]{2,1,0:T(8,128)S(1)}, u32[]{:S(2)}) %copy-start) | copy-done | bytes 26214424
  55.7 0.0 copy-start.1
  55.7 11.0 %fusion.11 = bf16[32,2,16,160]{3,0,2,1:T(8,128)(2,1)S(1)} fusion(f32[8,160,2560]{2,1,0:T(8,128)} %get-tuple-element.3, f32[8,160,2560]{2,1,0:T(8,128)} %get-tuple-element.2, f32[160]{0:T(256)S(1)} %dynamic_slice.7, bf16[32,1,2560]{2,0,1:T(8,128)(2,1)S(1)} %get-tuple-element.10, bf16[32,1,2560]{2,0,1:T(8,128)(2,1)S(1)} %get-tuple-element.11), kind=kOutput, calls=%fused_computation.15 | convolution fusion | flops 859504640 | bytes 26870400 | tf_op jit(solution)/shard_map/klx,mcx->mckl/dot_general | solution.py:70
  66.7 0.0 copy-start.2
  66.7 0.0 copy-start.4
  66.7 1.1 copy.11
  67.8 3.5 %all-to-all-start.1 = ((bf16[32,2,16,160]{3,2,1,0:T(8,128)(2,1)}), bf16[32,2,16,160]{3,2,1,0:T(8,128)(2,1)S(1)}, u32[]{:S(2)}, u32[]{:S(2)}) async-start(bf16[32,2,16,160]{3,2,1,0:T(8,128)(2,1)} %copy.11), calls=%async_computation.1 | async-start | bytes 1048576 | tf_op jit(solution)/shard_map/all_to_all | solution.py:76
  71.3 0.2 all-gather.2.cloned.1.call-start
  71.6 8.6 %all-to-all-done.1 = bf16[32,2,16,160]{3,2,1,0:T(8,128)(2,1)S(1)} async-done(((bf16[32,2,16,160]{3,2,1,0:T(8,128)(2,1)}), bf16[32,2,16,160]{3,2,1,0:T(8,128)(2,1)S(1)}, u32[]{:S(2)}, u32[]{:S(2)}) %all-to-all-start.1) | async-done | bytes 327712 | tf_op jit(solution)/shard_map/all_to_all | solution.py:76
  80.1 0.4 copy.17
  80.5 0.3 all_to_all.33
  80.8 4.9 %fusion.4 = f32[8,2,16,640]{3,2,1,0:T(8,128)S(1)} fusion(bf16[8,2,16,640]{3,2,1,0:T(8,128)(2,1)S(1)} %all_to_all.33, bf16[8,640,640]{2,1,0:T(8,128)(2,1)} %param.6), kind=kOutput, calls=%fused_computation.7 | convolution fusion | flops 209715200 | bytes 7536640 | tf_op jit(solution)/shard_map/mckl,mnl->mckn/dot_general | solution.py:74
  85.7 0.0 copy-done.1
  85.7 0.2 fusion.20
  85.9 0.9 pad_maximum_fusion
  86.8 0.0 all-gather.2.cloned.1.call-update
  86.9 0.0 copy-done.2
  86.9 0.7 fusion.32
  88.8 0.0 copy-done.4
  88.8 0.6 dynamic_slice.6
  89.4 0.6 iota_compare_fusion.4
  90.1 1.3 compare_and_fusion
  91.4 1.3 iota_compare_fusion
  92.7 2.0 %select_reduce_fusion.1 = f32[]{:T(128)} fusion(f32[640]{0:T(1024)S(1)} %copy-done.3, s32[]{:T(128)} %bitcast.19, s32[]{:T(128)} %bitcast.18), kind=kLoop, calls=%fused_computation.42 | loop fusion | flops 3199 | bytes 2572 | tf_op jit(solution)/shard_map/reduce_sum | solution.py:65
  94.7 3.0 %fusion.7 = f32[]{:T(128)} fusion(f32[16,160,2560]{2,1,0:T(8,128)} %copy-done, f32[160]{0:T(256)S(1)} %dynamic_slice.7, pred[2560]{0:T(1024)(128)(4,1)S(1)} %get-tuple-element.12, pred[2560]{0:T(1024)(128)(4,1)S(1)} %get-tuple-element.13, pred[160]{0:T(512)(128)(4,1)S(1)} %compare_and_fusion), kind=kLoop, calls=%fused_computation.12 | loop fusion | flops 2457599 | bytes 1644324 | tf_op jit(solution)/shard_map/reduce_sum | solution.py:61
  98.4 6.7 %psum.7 = f32[]{:T(128)} all-reduce(f32[]{:T(128)} %fusion.7), channel_id=1, replica_groups=mesh['member'=8,'wave'=4] {'wave'}, use_global_device_ids=true, to_apply=%region_2.3 | all-reduce | flops 1 | bytes 8 | tf_op jit(solution)/shard_map/psum | solution.py:62
  105.8 68.5 %all-gather.2.cloned.1.call-done = f32[8,8,32,640]{3,2,1,0:T(8,128)} async-done(((f32[1,8,32,640]{3,2,1,0:T(8,128)}), f32[8,8,32,640]{3,2,1,0:T(8,128)}) %all-gather.2.cloned.1.call-update) | async-done | bytes 5242896 | tf_op jit(solution)/shard_map/all_gather | solution.py:91
  174.3 4.0 %select_reduce_fusion = f32[8,32,640]{2,1,0:T(8,128)} fusion(f32[8,8,32,640]{3,2,1,0:T(8,128)} %all-gather.2.cloned.1.call-done, pred[8]{0:T(512)(128)(4,1)S(1)} %iota_compare_fusion.4), kind=kLoop, calls=%fused_computation.9 | loop fusion | flops 2457600 | bytes 5898248 | tf_op jit(solution)/shard_map/reduce_sum | solution.py:93
  (2 shorter events, 0.0 us)
Async XLA Ops:
  7.2 15.1 %copy-start.3 = (f32[640]{0:T(1024)S(1)}, f32[640]{0:T(1024)}, u32[]{:S(2)}) copy-start(f32[640]{0:T(1024)} %param.7) | copy-start | bytes 7684
  18.0 11.0 %all-to-all-start = ((bf16[4,2,20480]{2,1,0:T(2,128)(2,1)}), bf16[4,2,20480]{2,1,0:T(2,128)(2,1)S(1)}, u32[]{:S(2)}, u32[]{:S(2)}) async-start(bf16[4,2,20480]{2,1,0:T(2,128)(2,1)} %reshape.118), calls=%async_computation | async-start | bytes 655360 | tf_op jit(solution)/shard_map/all_to_all | solution.py:39
  39.2 16.5 %copy-start = (f32[16,160,2560]{2,1,0:T(8,128)}, f32[16,160,2560]{2,1,0:T(8,128)S(1)}, u32[]{:S(2)}) copy-start(f32[16,160,2560]{2,1,0:T(8,128)S(1)} %bitcast_multiply_fusion) | copy-start | bytes 78643200
  55.7 30.0 %copy-start.1 = (f32[1,8,32,640]{3,2,1,0:T(8,128)S(1)}, f32[1,8,32,640]{3,2,1,0:T(8,128)}, u32[]{:S(2)}) copy-start(f32[1,8,32,640]{3,2,1,0:T(8,128)} %param.5) | copy-start | bytes 1966084
  66.7 20.1 %copy-start.2 = (s32[4]{0:T(128)S(1)}, s32[4]{0:T(128)}, u32[]{:S(2)}) copy-start(s32[4]{0:T(128)} %param.8) | copy-start | bytes 52
  66.7 22.1 %copy-start.4 = (s32[8]{0:T(128)S(1)}, s32[8]{0:T(128)}, u32[]{:S(2)}) copy-start(s32[8]{0:T(128)} %param.9) | copy-start | bytes 100
  67.8 12.3 %all-to-all-start.1 = ((bf16[32,2,16,160]{3,2,1,0:T(8,128)(2,1)}), bf16[32,2,16,160]{3,2,1,0:T(8,128)(2,1)S(1)}, u32[]{:S(2)}, u32[]{:S(2)}) async-start(bf16[32,2,16,160]{3,2,1,0:T(8,128)(2,1)} %copy.11), calls=%async_computation.1 | async-start | bytes 1048576 | tf_op jit(solution)/shard_map/all_to_all | solution.py:76
  71.3 103.0 %all-gather.2.cloned.1.call-start = ((), (), s32[]{:S(2)}) async-start(), calls=%async_computation.2 | async-start | bytes 5898240 | tf_op jit(solution)/shard_map/all_gather | solution.py:91
Sparse Core Ops, SparseCore 0:
  87.0 87.2 all-gather.1
where the time goes:
time: 187 us; the launch traced here: 186 us
  waiting for transfers between devices  82.4 us (44%)
  other arithmetic  24.8 us (13%)
  matrix products  23.7 us (13%)
  local copies, waits for them, and re-layouts  22.8 us (12%)
  between operations  18 us (10%)
  starting transfers between devices  7.93 us (4%)
  blocking collectives  6.7 us (4%)
    all_gather x1, waiting for transfers between devices, on_device(): shards = lax.all_gather(stepped, 'member', axis=0, tiled=True)  68.5 us
    unnamed x12, local copies, waits for them, and re-layouts  11.7 us
    dot_general x1, matrix products, on_device(): jnp.einsum('klx,mcx->mckl', fluxes, fourier, preferred_element_type=jnp.f...  11 us
    mul x1, other arithmetic, on_device(): 0.5 * wind_grid * wind_grid  10.1 us
    all_to_all x1, waiting for transfers between devices, on_device(): lax.all_to_all(flux_coef, 'wave', split_axis=0, concat_axis=3, tiled=True)  8.55 us
    psum x1, blocking collectives, on_device(): region_total = lax.psum(region_part, 'wave')  6.7 us
    all_to_all x1, waiting for transfers between devices, on_device(): lax.all_to_all(fourier_coef, 'wave', split_axis=3, concat_axis=0, tiled=T...  5.27 us
    dot_general x1, matrix products, on_device(): jnp.einsum('mckl,mnl->mckn', lax.all_to_all(flux_coef, 'wave', split_axis...  4.88 us
  transfers between devices with their start and end apart: 3, of which 3 were waited for; matrix products, arithmetic and copies ran while one was open for 6% of the time, Pallas kernels for 0%

commit v1 on v0

v1 whole, which is shorter than its diff:
```python
import jax
import jax.numpy as jnp
import numpy as np
from jax import lax
from jax.sharding import PartitionSpec as P

NLON = 2560


advect_rate = 2.0


def wave_table(waves_total, points):
    wave_index = np.arange(waves_total)[:, None]
    angles = (wave_index * np.arange(points)[None, :] % points) * (2.0 * np.pi / points)
    return np.stack([np.cos(angles), -np.sin(angles)], axis=1)


def split_table(table):
    high = table.astype(jnp.bfloat16)
    low = (table - high.astype(np.float64)).astype(jnp.bfloat16)
    return high, low


def quadrature_points(waves_total):
    return (3 * (waves_total - 1)) // 128 * 128 + 128


def on_device(state, legendre, lat_weights, region, sources):
    wave_count = lax.axis_size("wave")
    waves_local = legendre.shape[0]
    waves_total = waves_local * wave_count
    degrees = legendre.shape[1]
    latitudes = legendre.shape[2]
    lat_rows = latitudes // wave_count
    state_rows = state.shape[2]
    level_count = state_rows // 4
    points = quadrature_points(waves_total)
    table_high, table_low = split_table(wave_table(waves_total, points))
    spectral = state[0]
    fourier_coef = jnp.einsum(
        "mrn,mnl->mrl", spectral.astype(jnp.bfloat16), legendre, preferred_element_type=jnp.float32
    )
    fourier_coef = fourier_coef.astype(jnp.bfloat16).reshape(
        waves_local, 2, 2 * level_count, latitudes
    )
    synthesis_scale = (2.0 * waves_total) ** (-0.5)
    coef = lax.all_to_all(fourier_coef, "wave", split_axis=3, concat_axis=0, tiled=True)
    gridded = synthesis_scale * jnp.einsum(
        "mckl,mcx->klx",
        jnp.concatenate([coef, coef], axis=1),
        jnp.concatenate([table_high, table_low], axis=1),
        preferred_element_type=jnp.float32,
    )
    lat_start = lax.axis_index("wave") * lat_rows
    local_weights = lax.dynamic_slice_in_dim(lat_weights, lat_start, lat_rows)
    wind_grid = gridded[:level_count]
    temper_grid = gridded[level_count:]
    fluxes = (
        jnp.concatenate([0.5 * wind_grid * wind_grid, wind_grid * temper_grid], axis=0)
        * local_weights[None, :, None]
    )
    fluxes = fluxes.astype(jnp.bfloat16)
    fourier = wave_table(waves_total, NLON).reshape(2 * waves_total, NLON).astype(jnp.bfloat16)
    lon_index = lax.broadcasted_iota(jnp.int32, (1, NLON), 1)
    lon_inside = (lon_index >= region[2]) & (lon_index < region[3])
    gram = jnp.einsum(
        "px,qx->pq",
        jnp.where(lon_inside, fourier, jnp.zeros((), jnp.bfloat16)),
        fourier,
        preferred_element_type=jnp.float32,
    )
    lowest = coef[:, :, -1].reshape(2 * waves_total, lat_rows).astype(jnp.float32)
    gram_lowest = jnp.dot(gram, lowest, precision=lax.Precision.HIGHEST)
    lat_index = lat_start + lax.broadcasted_iota(jnp.int32, (lat_rows,), 0)
    in_band = (lat_index >= region[0]) & (lat_index < region[1])
    region_part = jnp.sum(
        jnp.where(in_band, local_weights, 0.0)[None, :] * lowest * gram_lowest
    ) / (2.0 * waves_total)
    region_total = lax.psum(region_part, "wave")
    every_lat = lax.broadcasted_iota(jnp.int32, (latitudes,), 0)
    lat_inside = (every_lat >= region[0]) & (every_lat < region[1])
    region_weight = jnp.sum(jnp.where(lat_inside, lat_weights, 0.0)) * (
        region[3] - region[2]
    ).astype(jnp.float32)
    scores = (region_total / region_weight).reshape(1)
    analysis_scale = NLON ** (-0.5) * (NLON / points)
    flux_high = jnp.einsum("klx,mcx->mckl", fluxes, table_high, preferred_element_type=jnp.float32)
    flux_low = jnp.einsum("klx,mcx->mckl", fluxes, table_low, preferred_element_type=jnp.float32)
    flux_coef = (analysis_scale * (flux_high + flux_low)).astype(jnp.bfloat16)
    tendency = jnp.einsum(
        "mckl,mnl->mckn",
        lax.all_to_all(flux_coef, "wave", split_axis=0, concat_axis=3, tiled=True),
        legendre,
        preferred_element_type=jnp.float32,
    )
    wave_ids = lax.axis_index("wave") * waves_local + lax.broadcasted_iota(
        jnp.int32, (waves_local, 1, 1), 0
    )
    advection = advect_rate * wave_ids.astype(jnp.float32) / waves_total
    degree_ids = lax.broadcasted_iota(jnp.int32, (1, 1, degrees), 2).astype(jnp.float32)
    damping = 1.0 + ((degree_ids + 1.0) / degrees) ** 2
    spectral_split = spectral.reshape(waves_local, 2, 2 * level_count, degrees)
    real_part = (spectral_split[:, 0] + advection * tendency[:, 1]) / damping
    imag_part = (spectral_split[:, 1] - advection * tendency[:, 0]) / damping
    stepped = jnp.stack([real_part, imag_part], axis=1).reshape(1, waves_local, state_rows, degrees)
    source_member = sources[lax.axis_index("member")]
    shards = lax.all_gather(stepped.astype(jnp.bfloat16), "member", axis=0, tiled=True)
    cloned = lax.dynamic_slice_in_dim(shards, source_member, 1, axis=0).astype(jnp.float32)
    return (cloned, scores)


def solution(mesh):
    in_specs = (P("member", "wave", None, None), P("wave", None, None), P(), P(), P())
    out_specs = (P("member", "wave", None, None), P("member"))
    return jax.shard_map(
        on_device, mesh=mesh, in_specs=in_specs, out_specs=out_specs, check_vma=False
    )
```

time: 187 us -> 124 us (0.66)
  waiting for transfers between devices: 82.4 us -> 53.7 us
  other arithmetic: 24.8 us -> 7.19 us
  matrix products: 23.7 us -> 11.8 us
  local copies, waits for them, and re-layouts: 22.8 us -> 17.2 us
  between operations: 18 us -> 20.1 us
    all_gather x1, waiting for transfers between devices: 68.5 us -> 40.1 us  [on_device(): lax.all_gather(stepped.astype(jnp.bfloat16), 'member', axis=0, tiled=True)]
    dot_general x2 -> x5, matrix products: 14.6 us -> 2.67 us  [the longest x1 0.76 us: on_device(): gram_lowest = jnp.dot(gram, lowest, precision=lax.Precision.HIGHEST)]
    mul x1, other arithmetic: 10.1 us -> 0.12 us  [on_device(): 0.5 * wind_grid * wind_grid]
    reduce_sum x2 -> x0, other arithmetic: 7.02 us -> none  [the longest x1 3.99 us: on_device(): jnp.sum(jnp.where(owners == source_member, shards, 0.0), axis=0, keepdims...]
    unnamed x12 -> x18, local copies, waits for them, and re-layouts: 11.7 us -> 5.87 us
  transfers between devices with their start and end apart: 3 -> 3, of which waited for: 3 -> 3; matrix products, arithmetic and copies ran while one was open for 6% -> 5% of each run, Pallas kernels for 0% -> 0%
where the time goes in v1:
time: 124 us
  waiting for transfers between devices  53.7 us (43%)
  between operations  20.1 us (16%)
  local copies, waits for them, and re-layouts  17.2 us (14%)
  matrix products  11.8 us (10%)
  starting transfers between devices  7.75 us (6%)
  other arithmetic  7.19 us (6%)
  blocking collectives  6.27 us (5%)
    all_gather x1, waiting for transfers between devices, on_device(): lax.all_gather(stepped.astype(jnp.bfloat16), 'member', axis=0, tiled=True)  40.1 us
    all_to_all x1, waiting for transfers between devices, on_device(): lax.all_to_all(flux_coef, 'wave', split_axis=0, concat_axis=3, tiled=True)  8.73 us
    psum x1, blocking collectives, on_device(): region_total = lax.psum(region_part, 'wave')  6.27 us
    unnamed x18, local copies, waits for them, and re-layouts  5.87 us
    dot_general x1, matrix products, on_device(): jnp.einsum('mckl,mnl->mckn', lax.all_to_all(flux_coef, 'wave', split_axis...  4.95 us
    all_to_all x1, waiting for transfers between devices, on_device(): lax.all_to_all(fourier_coef, 'wave', split_axis=3, concat_axis=0, tiled=T...  4.84 us
    all_to_all x1, local copies, waits for them, and re-layouts, on_device(): lax.all_to_all(fourier_coef, 'wave', split_axis=3, concat_axis=0, tiled=T...  4.69 us
    all_to_all x1, starting transfers between devices, on_device(): lax.all_to_all(fourier_coef, 'wave', split_axis=3, concat_axis=0, tiled=T...  4.24 us
  transfers between devices with their start and end apart: 3, of which 3 were waited for; matrix products, arithmetic and copies ran while one was open for 5% of the time, Pallas kernels for 0%

profile of v1, /device:TPU:0, one launch (start us, length us, event | category | flops | bytes accessed | tf_op | source)
XLA Modules:
  0.0 124.0 jit_solution(11186973314322849637)
XLA Ops:
  7.2 4.2 %convolution_convert_fusion = bf16[8,32,640]{2,1,0:T(8,128)(2,1)S(1)} fusion(bf16[8,640,640]{2,1,0:T(8,128)(2,1)} %param.12, f32[1,8,32,640]{3,2,1,0:T(8,128)} %param.11), kind=kOutput, calls=%fused_computation.10 | convolution fusion | flops 210042880 | bytes 7536640 | tf_op jit(solution)/shard_map/mrn,mnl->mrl/dot_general | solution.py:41
  11.4 3.3 %copy.18 = bf16[8,2,16,640]{2,1,0,3:T(2,128)(2,1)S(1)} copy(bf16[8,2,16,640]{3,2,1,0:T(8,128)(2,1)S(1)} %bitcast.56) | data formatting | bytes 655360 | tf_op jit(solution)/shard_map/reshape | solution.py:44
  14.7 0.0 copy-start.3
  14.7 0.0 copy-start.4
  14.7 3.4 %reshape.69 = bf16[4,2,20480]{2,1,0:T(2,128)(2,1)} reshape(bf16[640,8,2,16]{3,2,1,0:T(2,128)(2,1)S(1)} %bitcast.53) | data formatting | bytes 655360
  18.1 4.2 %all-to-all-start = ((bf16[4,2,20480]{2,1,0:T(2,128)(2,1)}), bf16[4,2,20480]{2,1,0:T(2,128)(2,1)S(1)}, u32[]{:S(2)}, u32[]{:S(2)}) async-start(bf16[4,2,20480]{2,1,0:T(2,128)(2,1)} %reshape.69), calls=%async_computation | async-start | bytes 655360 | tf_op jit(solution)/shard_map/all_to_all | solution.py:48
  22.3 0.0 copy-done.3
  22.3 0.6 fusion.33
  22.9 0.0 copy-done.4
  22.9 1.3 %and_select_fusion = (f32[160]{0:T(256)S(1)}, f32[160]{0:T(256)S(1)}) fusion(s32[]{:T(128)} %bitcast.22, s32[]{:T(128)} %bitcast.21, s32[]{:T(128)S(6)} %mul.80, f32[640]{0:T(1024)S(1)} %copy-done.4, s32[]{:T(128)S(6)} %select_n.21), kind=kLoop, calls=%fused_computation.45 | loop fusion | flops 800 | bytes 1936 | tf_op jit(solution)/shard_map/jit(_where)/select_n | solution.py:78
  24.2 4.8 %all-to-all-done = bf16[4,2,20480]{2,1,0:T(2,128)(2,1)S(1)} async-done(((bf16[4,2,20480]{2,1,0:T(2,128)(2,1)}), bf16[4,2,20480]{2,1,0:T(2,128)(2,1)S(1)}, u32[]{:S(2)}, u32[]{:S(2)}) %all-to-all-start) | async-done | bytes 327712 | tf_op jit(solution)/shard_map/all_to_all | solution.py:48
  29.0 1.9 %reshape.70 = bf16[640,8,2,16]{3,2,1,0:T(2,128)(2,1)S(1)} reshape(bf16[4,2,20480]{2,1,0:T(2,128)(2,1)S(1)} %all-to-all-done) | data formatting | bytes 655360
  30.9 0.0 copy-start.7
  30.9 4.7 %copy.19 = bf16[8,2,16,4,160]{4,0,3,1,2:T(8,128)(2,1)S(1)} copy(bf16[8,2,16,4,160]{2,1,0,4,3:T(2,128)(2,1)S(1)} %bitcast.54) | data formatting | bytes 655360 | tf_op jit(solution)/shard_map/all_to_all | solution.py:48
  35.6 0.0 copy-done.7
  35.6 0.5 fusion.2
  36.1 0.0 copy-start.2
  36.1 0.1 multiply_multiply_fusion
  36.2 0.0 copy-start.1
  36.2 0.6 copy-done.2
  36.8 0.6 fusion.25
  37.4 0.0 copy-done.1
  37.4 0.6 fusion.6
  38.0 1.3 %copy.20 = bf16[32,2,16,160]{3,1,2,0:T(2,128)(2,1)} copy(bf16[32,2,16,160]{3,0,1,2:T(8,128)(2,1)S(1)} %fusion.6) | data formatting | bytes 655360 | tf_op jit(solution)/shard_map/convert_element_type | solution.py:90
  39.4 3.5 %all-to-all-start.1 = ((bf16[32,2,16,160]{3,1,2,0:T(2,128)(2,1)}), bf16[32,2,16,160]{3,1,2,0:T(2,128)(2,1)S(1)}, u32[]{:S(2)}, u32[]{:S(2)}) async-start(bf16[32,2,16,160]{3,1,2,0:T(2,128)(2,1)} %copy.20), calls=%async_computation.1 | async-start | bytes 1048576 | tf_op jit(solution)/shard_map/all_to_all | solution.py:93
  42.9 0.0 all-gather.2.cloned.1.call-start
  42.9 8.7 %all-to-all-done.1 = bf16[32,2,16,160]{3,1,2,0:T(2,128)(2,1)S(1)} async-done(((bf16[32,2,16,160]{3,1,2,0:T(2,128)(2,1)}), bf16[32,2,16,160]{3,1,2,0:T(2,128)(2,1)S(1)}, u32[]{:S(2)}, u32[]{:S(2)}) %all-to-all-start.1) | async-done | bytes 327712 | tf_op jit(solution)/shard_map/all_to_all | solution.py:93
  51.7 0.4 copy.27
  52.1 0.3 all_to_all.33
  52.4 0.0 copy-start
  52.4 4.9 %fusion = f32[8,2,16,640]{3,2,1,0:T(8,128)S(1)} fusion(bf16[8,2,16,640]{3,2,1,0:T(8,128)(2,1)S(1)} %all_to_all.33, bf16[8,640,640]{2,1,0:T(8,128)(2,1)} %param.12), kind=kOutput, calls=%fused_computation | convolution fusion | flops 209715200 | bytes 7536640 | tf_op jit(solution)/shard_map/mckl,mnl->mckn/dot_general | solution.py:91
  57.4 0.0 copy-done
  57.4 0.0 copy-start.5
  57.4 0.0 copy-start.6
  57.4 0.2 fusion.20
  57.6 0.8 pad_maximum_fusion
  58.3 0.0 all-gather.2.cloned.1.call-update
  58.4 0.0 copy-done.5
  58.4 0.6 dynamic_slice.10
  61.8 1.2 fusion.27
  63.0 1.8 %select_reduce_fusion = f32[]{:T(128)} fusion(f32[640]{0:T(1024)S(1)} %copy-done.4, s32[]{:T(128)} %bitcast.22, s32[]{:T(128)} %bitcast.21), kind=kLoop, calls=%fused_computation.40 | loop fusion | flops 3199 | bytes 2572 | tf_op jit(solution)/shard_map/reduce_sum | solution.py:83
  64.8 0.0 copy-done.6
  64.8 0.2 fusion.18
  65.1 0.8 fusion.11
  67.1 6.3 %psum.7 = f32[]{:T(128)} all-reduce(f32[]{:T(128)S(6)} %div.44), channel_id=1, replica_groups=mesh['member'=8,'wave'=4] {'wave'}, use_global_device_ids=true, to_apply=%region_1.2 | all-reduce | flops 1 | bytes 8 | tf_op jit(solution)/shard_map/psum | solution.py:80
  74.0 40.1 %all-gather.2.cloned.1.call-done = bf16[8,8,32,640]{3,2,1,0:T(8,128)(2,1)} async-done(((bf16[1,8,32,640]{3,2,1,0:T(8,128)(2,1)}), bf16[8,8,32,640]{3,2,1,0:T(8,128)(2,1)}) %all-gather.2.cloned.1.call-update) | async-done | bytes 2621456 | tf_op jit(solution)/shard_map/all_gather | solution.py:108
  114.1 1.9 %dynamic-slice_convert_fusion = f32[1,8,32,640]{3,2,1,0:T(8,128)} fusion(bf16[8,8,32,640]{3,2,1,0:T(8,128)(2,1)} %all-gather.2.cloned.1.call-done, s32[]{:T(128)S(6)} %select_n.23), kind=kLoop, calls=%fused_computation.28 | loop fusion | flops 163840 | bytes 983044 | tf_op jit(solution)/shard_map/convert_element_type | solution.py:109
  (5 shorter events, 0.1 us)
Async XLA Ops:
  14.7 7.6 %copy-start.3 = (s32[4]{0:T(128)S(1)}, s32[4]{0:T(128)}, u32[]{:S(2)}) copy-start(s32[4]{0:T(128)} %param.14) | copy-start | bytes 52
  14.7 8.2 %copy-start.4 = (f32[640]{0:T(1024)S(1)}, f32[640]{0:T(1024)}, u32[]{:S(2)}) copy-start(f32[640]{0:T(1024)} %param.13) | copy-start | bytes 7684
  18.1 11.0 %all-to-all-start = ((bf16[4,2,20480]{2,1,0:T(2,128)(2,1)}), bf16[4,2,20480]{2,1,0:T(2,128)(2,1)S(1)}, u32[]{:S(2)}, u32[]{:S(2)}) async-start(bf16[4,2,20480]{2,1,0:T(2,128)(2,1)} %reshape.69), calls=%async_computation | async-start | bytes 655360 | tf_op jit(solution)/shard_map/all_to_all | solution.py:48
  30.9 4.7 %copy-start.7 = (bf16[32,4,128,1]{2,0,1,3:T(8,128)(2,1)S(1)}, bf16[32,4,128,1]{2,0,1,3:T(8,128)(2,1)}, u32[]{:S(2)}) copy-start(bf16[32,4,128,1]{2,0,1,3:T(8,128)(2,1)} %constant.51) | copy-start | bytes 98308
  36.1 0.7 copy-start.2
  36.2 1.2 copy-start.1
  39.4 12.3 %all-to-all-start.1 = ((bf16[32,2,16,160]{3,1,2,0:T(2,128)(2,1)}), bf16[32,2,16,160]{3,1,2,0:T(2,128)(2,1)S(1)}, u32[]{:S(2)}, u32[]{:S(2)}) async-start(bf16[32,2,16,160]{3,1,2,0:T(2,128)(2,1)} %copy.20), calls=%async_computation.1 | async-start | bytes 1048576 | tf_op jit(solution)/shard_map/all_to_all | solution.py:93
  42.9 71.3 %all-gather.2.cloned.1.call-start = ((), (), s32[]{:S(2)}) async-start(), calls=%async_computation.2 | async-start | bytes 2949120 | tf_op jit(solution)/shard_map/all_gather | solution.py:108
  52.4 5.0 %copy-start = (f32[1,8,32,640]{3,2,1,0:T(8,128)S(1)}, f32[1,8,32,640]{3,2,1,0:T(8,128)}, u32[]{:S(2)}) copy-start(f32[1,8,32,640]{3,2,1,0:T(8,128)} %param.11) | copy-start | bytes 1966084
  57.4 1.0 copy-start.5
  57.4 7.4 %copy-start.6 = (bf16[64,2560]{1,0:T(8,128)(2,1)S(1)}, bf16[64,2560]{1,0:T(8,128)(2,1)}, u32[]{:S(2)}) copy-start(bf16[64,2560]{1,0:T(8,128)(2,1)} %constant.48.clone) | copy-start | bytes 983044
Sparse Core Ops, SparseCore 0:
  58.5 55.5 all-gather.1

commit v2 on v1

--- a/solution.py
+++ b/solution.py
@@ -1,7 +1,11 @@
+import functools
+
 import jax
 import jax.numpy as jnp
 import numpy as np
 from jax import lax
+from jax.experimental import pallas as pl
+from jax.experimental.pallas import tpu as pltpu
 from jax.sharding import PartitionSpec as P
 
 NLON = 2560
@@ -110,9 +114,389 @@
     return (cloned, scores)
 
 
+MESH = pl.DeviceIdType.MESH
+WAVES = 4
+CHUNKS = 4
+PAIR = 2
+ROWS = 32
+CHUNK_ROWS = PAIR * ROWS
+PART_ROWS = CHUNK_ROWS // WAVES
+OWNED_ROWS = CHUNKS * PART_ROWS
+
+
+def order_tables(levels):
+    held = levels // WAVES
+    forward = np.zeros((CHUNK_ROWS, CHUNK_ROWS))
+    backward = np.zeros((CHUNK_ROWS, CHUNK_ROWS))
+    for m in range(PAIR):
+        for c in range(2):
+            for f in range(2):
+                for k in range(levels):
+                    plain = ((m * 2 + c) * 2 + f) * levels + k
+                    owner = ((((k // held) * PAIR + m) * 2 + c) * 2 + f) * held + k % held
+                    crossed = ((((k // held) * PAIR + m) * 2 + (1 - c)) * 2 + f) * held + k % held
+                    forward[owner, plain] = 1.0
+                    backward[plain, crossed] = 1.0 - 2.0 * c
+    return forward.astype(jnp.bfloat16), backward.astype(jnp.bfloat16)
+
+
+def grid_tables(table):
+    waves, _, points = table.shape
+    wide = np.einsum("mcx,fg,kl->lgxmcfk", table, np.eye(2), np.eye(2))
+    return split_table(wide.reshape(4 * points, 8 * waves))
+
+
+def step_kernel(
+    state_ref, legendre_ref, weights_ref, region_ref, sources_ref, synth_ref, analysis_ref,
+    forward_ref, backward_ref, pick_ref, fourier_ref,
+    out_ref, score_ref,
+    leg, sent, held, flux, back_sent, back, score_buf, cross, crossed,
+    pool0, pool1, pool2, pool3,
+    leg_sem, go_send, go_recv, ret_send, ret_recv, score_send, score_recv,
+    pass_send, pass_recv, cross_send, cross_recv,
+    *, scale, analysis_scale, waves_total,
+):
+    pools = [pool0, pool1, pool2, pool3]
+    me = lax.axis_index("wave")
+    slot = lax.axis_index("member")
+    z = slot // 2
+    x = slot % 2
+    half = z // 2
+    inner = z % 2 != half % 2
+    z_mate = (z + 1 - 2 * (z % 2)) * 2 + x
+    x_mate = z * 2 + 1 - x
+    far_inner = (2 - half) * 2 + x
+    far_outer = (3 - 3 * half) * 2 + x
+    here = slot - half * 4
+    z_here = z_mate - half * 4
+    points = synth_ref.shape[1] // 4
+    degrees = state_ref.shape[1]
+    lat_count = weights_ref.shape[1]
+
+    loads = [
+        pltpu.make_async_copy(legendre_ref.at[m], leg.at[m], leg_sem.at[m])
+        for m in range(CHUNKS * PAIR)
+    ]
+    for load in loads:
+        load.start()
+
+    barrier = pltpu.get_barrier_semaphore()
+    for d in range(1, WAVES):
+        pl.semaphore_signal(
+            barrier, inc=1, device_id={"wave": (me + d) % WAVES}, device_id_type=MESH
+        )
+    for mate in (z_mate, x_mate, far_inner):
+        pl.semaphore_signal(barrier, inc=1, device_id={"member": mate}, device_id_type=MESH)
+
+    @pl.when(inner)
+    def _():
+        pl.semaphore_signal(barrier, inc=1, device_id={"member": far_outer}, device_id_type=MESH)
+        pl.semaphore_wait(barrier, 7)
+
+    @pl.when(jnp.logical_not(inner))
+    def _():
+        pl.semaphore_wait(barrier, 6)
+
+    def wave_copy(source, target, target_row, c, d, send_sem, recv_sem):
+        to = (me + d) % WAVES
+        return pltpu.make_async_remote_copy(
+            src_ref=source.at[pl.ds(pl.multiple_of(to * OWNED_ROWS + c * PART_ROWS, PART_ROWS), PART_ROWS)],
+            dst_ref=target.at[pl.ds(pl.multiple_of(target_row, PART_ROWS), PART_ROWS)],
+            send_sem=send_sem.at[d - 1, c],
+            recv_sem=recv_sem.at[d - 1, c],
+            device_id={"wave": to},
+            device_id_type=MESH,
+        )
+
+    my_rows = me * OWNED_ROWS
+    go = []
+    for c in range(CHUNKS):
+        parts = []
+        for m in range(c * PAIR, (c + 1) * PAIR):
+            loads[m].wait()
+            parts.append(
+                jnp.dot(
+                    state_ref[m * ROWS : (m + 1) * ROWS].astype(jnp.bfloat16),
+                    leg[m],
+                    preferred_element_type=jnp.float32,
+                )
+            )
+        coef = jnp.concatenate(parts, axis=0).astype(jnp.bfloat16)
+        ordered = jnp.dot(
+            forward_ref[...], coef, preferred_element_type=jnp.float32
+        ).astype(jnp.bfloat16)
+        for w in range(WAVES):
+            sent[w * OWNED_ROWS + c * PART_ROWS : w * OWNED_ROWS + (c + 1) * PART_ROWS] = ordered[
+                w * PART_ROWS : (w + 1) * PART_ROWS
+            ]
+        for d in (2, 1, 3):
+            copy = wave_copy(sent, held, my_rows + c * PART_ROWS, c, d, go_send, go_recv)
+            copy.start()
+            go.append(copy)
+    mine = pl.ds(pl.multiple_of(my_rows, OWNED_ROWS), OWNED_ROWS)
+    held[mine] = sent[mine]
+
+    low, high = region_ref[2], region_ref[3]
+    lon = lax.broadcasted_iota(jnp.int32, (1, fourier_ref.shape[1]), 1)
+    lon_inside = jnp.where((lon >= low) & (lon < high), 1.0, 0.0)
+    fourier = fourier_ref[...]
+    gram = lax.dot_general(
+        (fourier.astype(jnp.float32) * lon_inside).astype(jnp.bfloat16),
+        fourier,
+        (((1,), (1,)), ((), ())),
+        preferred_element_type=jnp.float32,
+    )
+    gram_high = gram.astype(jnp.bfloat16)
+    gram_low = (gram - gram_high.astype(jnp.float32)).astype(jnp.bfloat16)
+    lat = lax.broadcasted_iota(jnp.int32, (1, lat_count), 1)
+    weights = weights_ref[...]
+    region_weights = jnp.where((lat >= region_ref[0]) & (lat < region_ref[1]), weights, 0.0)
+    weight_sum = jnp.sum(region_weights, axis=1, keepdims=True) * (high - low).astype(jnp.float32)
+
+    for copy in go:
+        copy.wait_recv()
+
+    coefs = held[...]
+    scaled = weights * (scale * scale)
+    for k in range(2):
+        rows = slice(k * 2 * points, (k + 1) * 2 * points)
+        grid = jnp.dot(
+            synth_ref[0, rows], coefs, preferred_element_type=jnp.float32
+        ) + jnp.dot(synth_ref[1, rows], coefs, preferred_element_type=jnp.float32)
+        wind = grid[:points]
+        weighted = wind * scaled
+        flux[k * 2 * points : (k * 2 + 1) * points] = (0.5 * weighted * wind).astype(jnp.bfloat16)
+        flux[(k * 2 + 1) * points : (k * 2 + 2) * points] = (weighted * grid[points:]).astype(
+            jnp.bfloat16
+        )
+    fluxes = flux[...]
+    back_sent[...] = (
+        analysis_scale
+        * (
+            jnp.dot(analysis_ref[0], fluxes, preferred_element_type=jnp.float32)
+            + jnp.dot(analysis_ref[1], fluxes, preferred_element_type=jnp.float32)
+        )
+    ).astype(jnp.bfloat16)
+    ret = []
+    for c in range(CHUNKS):
+        for d in (2, 1, 3):
+            copy = wave_copy(back_sent, back, my_rows + c * PART_ROWS, c, d, ret_send, ret_recv)
+            copy.start()
+            ret.append(copy)
+    back[mine] = back_sent[mine]
+
+    lowest = jnp.dot(pick_ref[...], coefs, preferred_element_type=jnp.float32)
+    lowest_half = lowest.astype(jnp.bfloat16)
+    spread = jnp.dot(gram_high, lowest_half, preferred_element_type=jnp.float32) + jnp.dot(
+        gram_low, lowest_half, preferred_element_type=jnp.float32
+    )
+    squares = jnp.sum(lowest * spread, axis=0, keepdims=True) * (region_weights * (scale * scale))
+    score = jnp.sum(squares, axis=1, keepdims=True) / weight_sum
+    score = score * jnp.where(me == WAVES - 1, 1.0, 0.0)
+    score_buf[me] = jnp.broadcast_to(score, score_buf.shape[1:])
+    score_copies = []
+    for d in range(1, WAVES):
+        copy = pltpu.make_async_remote_copy(
+            src_ref=score_buf.at[me],
+            dst_ref=score_buf.at[me],
+            send_sem=score_send.at[d - 1],
+            recv_sem=score_recv.at[d - 1],
+            device_id={"wave": (me + d) % WAVES},
+            device_id_type=MESH,
+        )
+        copy.start()
+        score_copies.append(copy)
+
+    def member_copy(source, target, to, send_sem, recv_sem):
+        return pltpu.make_async_remote_copy(
+            src_ref=source, dst_ref=target, send_sem=send_sem, recv_sem=recv_sem,
+            device_id={"member": to}, device_id_type=MESH,
+        )
+
+    def pass_copy(c, kind):
+        which = z_here if kind == 2 else here
+        block = pools[c].at[which]
+        return member_copy(
+            block, block, z_mate if kind == 0 else x_mate, pass_send.at[kind, c], pass_recv.at[kind, c]
+        )
+
+    def cross_copy(c, far):
+        return member_copy(
+            cross.at[c, far],
+            crossed.at[c],
+            far_outer if far else far_inner,
+            cross_send.at[far, c],
+            cross_recv.at[c],
+        )
+
+    def half_index(member_slot):
+        return jnp.clip(sources_ref[member_slot] - half * 4, 0, 3)
+
+    inner_pick = half_index(far_inner)
+    outer_pick = half_index(far_outer)
+
+    def forward_pass(c):
+        pass_copy(c, 0).wait_recv()
+        pass_copy(c, 2).start()
+
+    def send_across(c):
+        pass_copy(c, 1).wait_recv()
+        pass_copy(c, 2).wait_recv()
+
+        @pl.when(inner)
+        def _():
+            cross[c, 1] = pools[c][outer_pick]
+            cross_copy(c, 1).start()
+            cross[c, 0] = pools[c][inner_pick]
+            cross_copy(c, 0).start()
+
+    degree = lax.broadcasted_iota(jnp.int32, (1, degrees), 1).astype(jnp.float32)
+    keep = 1.0 / (1.0 + ((degree + 1.0) / degrees) ** 2)
+    for c in range(CHUNKS):
+        for copy in ret[c * (WAVES - 1) : (c + 1) * (WAVES - 1)]:
+            copy.wait_recv()
+        arrived = jnp.concatenate(
+            [
+                back[w * OWNED_ROWS + c * PART_ROWS : w * OWNED_ROWS + (c + 1) * PART_ROWS]
+                for w in range(WAVES)
+            ],
+            axis=0,
+        )
+        plain = jnp.dot(
+            backward_ref[...], arrived, preferred_element_type=jnp.float32
+        ).astype(jnp.bfloat16)
+        for i in range(PAIR):
+            m = c * PAIR + i
+            tendency = lax.dot_general(
+                plain[i * ROWS : (i + 1) * ROWS],
+                leg[m],
+                (((1,), (1,)), ((), ())),
+                preferred_element_type=jnp.float32,
+            )
+            wave_id = (me * (CHUNKS * PAIR) + m).astype(jnp.float32)
+            advection = wave_id * (advect_rate / waves_total)
+            stepped = (state_ref[m * ROWS : (m + 1) * ROWS] + advection * tendency) * keep
+            pools[c][here, i * ROWS : (i + 1) * ROWS] = stepped.astype(jnp.bfloat16)
+        pass_copy(c, 0).start()
+        pass_copy(c, 1).start()
+        if c >= 1:
+            forward_pass(c - 1)
+        if c >= 3:
+            send_across(c - 3)
+    forward_pass(CHUNKS - 1)
+    for c in range(CHUNKS - 3, CHUNKS):
+        send_across(c)
+
+    for copy in score_copies:
+        copy.wait()
+    score_ref[...] = score_buf[0] + score_buf[1] + score_buf[2] + score_buf[3]
+    for copy in go + ret:
+        copy.wait_send()
+
+    origin = sources_ref[slot] - half * 4
+    near = (origin >= 0) & (origin < 4)
+    choice = jnp.clip(origin, 0, 3)
+    for c in range(CHUNKS):
+        cross_copy(c, 0).wait_recv()
+        out_ref[c * CHUNK_ROWS : (c + 1) * CHUNK_ROWS] = jnp.where(
+            near, pools[c][choice], crossed[c]
+        )
+    for c in range(CHUNKS):
+        for kind in range(3):
+            pass_copy(c, kind).wait_send()
+
+    @pl.when(inner)
+    def _():
+        for c in range(CHUNKS):
+            for far in range(2):
+                cross_copy(c, far).wait_send()
+
+
+def in_one_kernel(state, legendre, lat_weights, region, sources):
+    waves_local, degrees, latitudes = legendre.shape
+    waves_total = waves_local * WAVES
+    points = quadrature_points(waves_total)
+    levels = state.shape[2] // 4
+    synth_high, synth_low = grid_tables(wave_table(waves_total, points))
+    forward, backward = order_tables(levels)
+    pick = np.zeros((2 * waves_total, 8 * waves_total))
+    pick[np.arange(2 * waves_total), np.arange(2 * waves_total) * 4 + 3] = 1.0
+    fourier = wave_table(waves_total, NLON).reshape(2 * waves_total, NLON).astype(jnp.bfloat16)
+    vmem = pl.BlockSpec(memory_space=pltpu.VMEM)
+    smem = pl.BlockSpec(memory_space=pltpu.SMEM)
+    rows = waves_local * ROWS
+    block = (rows, degrees)
+    dma = pltpu.SemaphoreType.DMA
+    cloned, scores = pl.pallas_call(
+        functools.partial(
+            step_kernel,
+            scale=(2.0 * waves_total) ** -0.5,
+            analysis_scale=NLON**-0.5 * (NLON / points),
+            waves_total=waves_total,
+        ),
+        out_shape=(
+            jax.ShapeDtypeStruct(block, jnp.bfloat16),
+            jax.ShapeDtypeStruct((8, 128), jnp.float32),
+        ),
+        in_specs=[vmem, pl.BlockSpec(memory_space=pl.ANY), vmem, smem, smem] + [vmem] * 6,
+        out_specs=(vmem, vmem),
+        scratch_shapes=[
+            pltpu.VMEM(legendre.shape, jnp.bfloat16),
+            pltpu.VMEM((rows, latitudes), jnp.bfloat16),
+            pltpu.VMEM((rows, latitudes), jnp.bfloat16),
+            pltpu.VMEM((4 * points, latitudes), jnp.bfloat16),
+            pltpu.VMEM((rows, latitudes), jnp.bfloat16),
+            pltpu.VMEM((rows, latitudes), jnp.bfloat16),
+            pltpu.VMEM((WAVES, 8, 128), jnp.float32),
+            pltpu.VMEM((CHUNKS, 2, CHUNK_ROWS, degrees), jnp.bfloat16),
+            pltpu.VMEM((CHUNKS, CHUNK_ROWS, degrees), jnp.bfloat16),
+        ]
+        + [pltpu.VMEM((4, CHUNK_ROWS, degrees), jnp.bfloat16)] * CHUNKS
+        + [
+            dma((waves_local,)),
+            dma((WAVES - 1, CHUNKS)),
+            dma((WAVES - 1, CHUNKS)),
+            dma((WAVES - 1, CHUNKS)),
+            dma((WAVES - 1, CHUNKS)),
+            dma((WAVES - 1,)),
+            dma((WAVES - 1,)),
+            dma((3, CHUNKS)),
+            dma((3, CHUNKS)),
+            dma((2, CHUNKS)),
+            dma((CHUNKS,)),
+        ],
+        compiler_params=pltpu.CompilerParams(
+            collective_id=0, has_side_effects=True, vmem_limit_bytes=48 * 1024 * 1024
+        ),
+    )(
+        state.reshape(block),
+        legendre,
+        lat_weights.reshape(1, latitudes),
+        region,
+        sources,
+        jnp.asarray(np.stack([synth_high, synth_low])),
+        jnp.asarray(np.stack([synth_high.T, synth_low.T])),
+        jnp.asarray(forward),
+        jnp.asarray(backward),
+        jnp.asarray(pick.astype(jnp.bfloat16)),
+        jnp.asarray(fourier),
+    )
+    return (cloned.astype(jnp.float32).reshape(state.shape), scores[0, :1])
+
+
 def solution(mesh):
     in_specs = (P("member", "wave", None, None), P("wave", None, None), P(), P(), P())
     out_specs = (P("member", "wave", None, None), P("member"))
-    return jax.shard_map(
-        on_device, mesh=mesh, in_specs=in_specs, out_specs=out_specs, check_vma=False
-    )
+
+    def run(state, legendre, lat_weights, region, sources):
+        shape = (state.shape[1] // mesh.shape["wave"], state.shape[2], state.shape[3], legendre.shape[2])
+        fits = mesh.shape["wave"] == 4 and mesh.shape["member"] == 8 and shape == (8, 32, 640, 640)
+        return jax.shard_map(
+            in_one_kernel if fits else on_device,
+            mesh=mesh,
+            in_specs=in_specs,
+            out_specs=out_specs,
+            check_vma=False,
+        )(state, legendre, lat_weights, region, sources)
+
+    return run

time: 124 us -> 51.3 us (0.41)
  waiting for transfers between devices: 53.7 us -> 0 us
  Pallas kernels: 0 us -> 40.4 us
  between operations: 20.1 us -> 0.65 us
  matrix products: 11.8 us -> 0 us
  local copies, waits for them, and re-layouts: 17.2 us -> 8.84 us
  starting transfers between devices: 7.75 us -> 0 us
  other arithmetic: 7.19 us -> 0.89 us
  blocking collectives: 6.27 us -> 0 us
    pallas_call x0 -> x1, Pallas kernels: none -> 40.4 us  [in_one_kernel(): pl.pallas_call(functools.partial(step_kernel, scale=(2.0 * waves_total) *...]
    all_gather x1 -> x0, waiting for transfers between devices: 40.1 us -> none  [on_device(): lax.all_gather(stepped.astype(jnp.bfloat16), 'member', axis=0, tiled=True)]
    all_to_all x2 -> x0, waiting for transfers between devices: 13.6 us -> none  [the longest x1 8.73 us: on_device(): lax.all_to_all(flux_coef, 'wave', split_axis=0, concat_axis=3, tiled=True)]
    dot_general x7 -> x0, matrix products: 11.8 us -> none  [the longest x1 4.95 us: on_device(): jnp.einsum('mckl,mnl->mckn', lax.all_to_all(flux_coef, 'wave', split_axis...]
    all_to_all x2 -> x0, starting transfers between devices: 7.71 us -> none  [the longest x1 4.24 us: on_device(): lax.all_to_all(fourier_coef, 'wave', split_axis=3, concat_axis=0, tiled=T...]
    psum x1 -> x0, blocking collectives: 6.27 us -> none  [on_device(): region_total = lax.psum(region_part, 'wave')]
    all_to_all x3 -> x0, local copies, waits for them, and re-layouts: 5.42 us -> none  [the longest x1 4.69 us: on_device(): lax.all_to_all(fourier_coef, 'wave', split_axis=3, concat_axis=0, tiled=T...]
    reshape x1, local copies, waits for them, and re-layouts: 3.3 us -> 0.69 us  [in_one_kernel(): lat_weights.reshape(1, latitudes)]
  transfers between devices with their start and end apart: 3 -> 0, of which waited for: 3 -> 0; matrix products, arithmetic and copies ran while one was open for 5% -> 0% of each run, Pallas kernels for 0% -> 0%
where the time goes in v2:
time: 51.3 us; the launch traced here: 50.8 us
  Pallas kernels  40.4 us (79%)
  local copies, waits for them, and re-layouts  8.84 us (17%)
  other arithmetic  0.89 us (2%)
  between operations  0.65 us (1%)
    pallas_call x1, Pallas kernels, in_one_kernel(): pl.pallas_call(functools.partial(step_kernel, scale=(2.0 * waves_total) *...  40.4 us
    unnamed x18, local copies, waits for them, and re-layouts  7.64 us

profile of v2, /device:TPU:0, one launch (start us, length us, event | category | flops | bytes accessed | tf_op | source)
XLA Modules:
  0.0 50.8 jit_solution(4415240255142769178)
XLA Ops:
  0.6 0.7 %reshape.17.weights_ref = f32[1,640]{1,0:T(1,128)S(1)} reshape(f32[640]{0:T(1024)} %param.13) | data formatting | bytes 5120 | tf_op jit(solution)/shard_map/reshape | solution.py:474
  1.3 0.0 copy-start
  1.3 1.1 %copy-done = f32[1,8,32,640]{3,2,1,0:T(8,128)S(1)} copy-done((f32[1,8,32,640]{3,2,1,0:T(8,128)S(1)}, f32[1,8,32,640]{3,2,1,0:T(8,128)}, u32[]{:S(2)}) %copy-start) | copy-done | bytes 655384
  2.4 0.0 copy-start.1
  2.4 1.0 %copy-done.1 = bf16[2,256,512]{2,1,0:T(8,128)(2,1)S(1)} copy-done((bf16[2,256,512]{2,1,0:T(8,128)(2,1)S(1)}, bf16[2,256,512]{2,1,0:T(8,128)(2,1)}, u32[]{:S(2)}) %copy-start.1) | copy-done | bytes 524312
  3.4 0.0 copy-start.2
  3.5 1.0 %copy-done.2 = bf16[2,512,256]{2,1,0:T(8,128)(2,1)S(1)} copy-done((bf16[2,512,256]{2,1,0:T(8,128)(2,1)S(1)}, bf16[2,512,256]{2,1,0:T(8,128)(2,1)}, u32[]{:S(2)}) %copy-start.2) | copy-done | bytes 524312
  4.5 0.0 copy-start.3
  4.5 1.0 %copy-done.3 = bf16[64,2560]{1,0:T(8,128)(2,1)S(1)} copy-done((bf16[64,2560]{1,0:T(8,128)(2,1)S(1)}, bf16[64,2560]{1,0:T(8,128)(2,1)}, u32[]{:S(2)}) %copy-start.3) | copy-done | bytes 327704
  5.5 0.0 copy-start.4
  5.5 0.8 %copy-done.4 = bf16[64,256]{1,0:T(8,128)(2,1)S(1)} copy-done((bf16[64,256]{1,0:T(8,128)(2,1)S(1)}, bf16[64,256]{1,0:T(8,128)(2,1)}, u32[]{:S(2)}) %copy-start.4) | copy-done | bytes 32792
  6.2 0.0 copy-start.5
  6.2 0.7 %copy-done.5 = bf16[64,64]{1,0:T(8,128)(2,1)S(1)} copy-done((bf16[64,64]{1,0:T(8,128)(2,1)S(1)}, bf16[64,64]{1,0:T(8,128)(2,1)}, u32[]{:S(2)}) %copy-start.5) | copy-done | bytes 8216
  6.9 0.0 copy-start.6
  6.9 0.7 %copy-done.6 = bf16[64,64]{1,0:T(8,128)(2,1)S(1)} copy-done((bf16[64,64]{1,0:T(8,128)(2,1)S(1)}, bf16[64,64]{1,0:T(8,128)(2,1)}, u32[]{:S(2)}) %copy-start.6) | copy-done | bytes 8216
  7.7 0.0 copy-start.7
  7.7 0.7 %copy-done.7 = s32[4]{0:T(128)S(1)} copy-done((s32[4]{0:T(128)S(1)}, s32[4]{0:T(128)}, u32[]{:S(2)}) %copy-start.7) | copy-done | bytes 40
  8.3 0.0 copy-start.8
  8.3 0.7 %copy-done.8 = s32[8]{0:T(128)S(1)} copy-done((s32[8]{0:T(128)S(1)}, s32[8]{0:T(128)}, u32[]{:S(2)}) %copy-start.8) | copy-done | bytes 56
  9.0 40.4 %shard_map.122 = (bf16[256,640]{1,0:T(8,128)(2,1)S(1)}, f32[8,128]{1,0:T(8,128)S(1)}) custom-call(f32[256,640]{1,0:T(8,128)S(1)} %bitcast.4, bf16[8,640,640]{2,1,0:T(8,128)(2,1)} %legendre_ref.1, f32[1,640]{1,0:T(1,128)S(1)} %reshape.17.weights_ref, s32[4]{0:T(128)S(1)} %copy-done.7, s32[8]{0:T(128)S(1)} %copy-done.8, bf16[2,512,256]{2,1,0:T(8,128)(2,1)S(1)} %copy-done.2, ...), custom_call_target="tpu_custom_call" | custom-call | tf_op jit(solution)/shard_map/pallas_call | solution.py:430
  49.4 0.5 %slice.3 = f32[1,1]{1,0:T(1,128)} slice(f32[8,128]{1,0:T(8,128)S(1)} %get-tuple-element.5), slice={[0:1], [0:1]} | slice | bytes 8 | tf_op jit(solution)/shard_map/slice | solution.py:484
  49.9 0.9 %convert.1 = f32[1,8,32,640]{3,2,1,0:T(8,128)} convert(bf16[1,8,32,640]{3,2,1,0:T(8,128)(2,1)S(1)} %bitcast.5) | non-fusion elementwise | flops 163840 | bytes 983040 | tf_op jit(solution)/shard_map/reshape | solution.py:484
Async XLA Ops:
  1.3 1.1 %copy-start = (f32[1,8,32,640]{3,2,1,0:T(8,128)S(1)}, f32[1,8,32,640]{3,2,1,0:T(8,128)}, u32[]{:S(2)}) copy-start(f32[1,8,32,640]{3,2,1,0:T(8,128)} %param.11) | copy-start | bytes 1966084
  2.4 1.0 %copy-start.1 = (bf16[2,256,512]{2,1,0:T(8,128)(2,1)S(1)}, bf16[2,256,512]{2,1,0:T(8,128)(2,1)}, u32[]{:S(2)}) copy-start(bf16[2,256,512]{2,1,0:T(8,128)(2,1)} %constant.13.clone.analysis_ref) | copy-start | bytes 1572868
  3.4 1.0 %copy-start.2 = (bf16[2,512,256]{2,1,0:T(8,128)(2,1)S(1)}, bf16[2,512,256]{2,1,0:T(8,128)(2,1)}, u32[]{:S(2)}) copy-start(bf16[2,512,256]{2,1,0:T(8,128)(2,1)} %constant.12.clone.synth_ref) | copy-start | bytes 1572868
  4.5 1.0 %copy-start.3 = (bf16[64,2560]{1,0:T(8,128)(2,1)S(1)}, bf16[64,2560]{1,0:T(8,128)(2,1)}, u32[]{:S(2)}) copy-start(bf16[64,2560]{1,0:T(8,128)(2,1)} %constant.17.clone.fourier_ref) | copy-start | bytes 983044
  5.5 0.8 %copy-start.4 = (bf16[64,256]{1,0:T(8,128)(2,1)S(1)}, bf16[64,256]{1,0:T(8,128)(2,1)}, u32[]{:S(2)}) copy-start(bf16[64,256]{1,0:T(8,128)(2,1)} %constant.16.clone.pick_ref) | copy-start | bytes 98308
  6.2 0.7 %copy-start.5 = (bf16[64,64]{1,0:T(8,128)(2,1)S(1)}, bf16[64,64]{1,0:T(8,128)(2,1)}, u32[]{:S(2)}) copy-start(bf16[64,64]{1,0:T(8,128)(2,1)} %constant.15.clone.backward_ref) | copy-start | bytes 24580
  6.9 0.7 %copy-start.6 = (bf16[64,64]{1,0:T(8,128)(2,1)S(1)}, bf16[64,64]{1,0:T(8,128)(2,1)}, u32[]{:S(2)}) copy-start(bf16[64,64]{1,0:T(8,128)(2,1)} %constant.14.clone.forward_ref) | copy-start | bytes 24580
  7.7 0.7 %copy-start.7 = (s32[4]{0:T(128)S(1)}, s32[4]{0:T(128)}, u32[]{:S(2)}) copy-start(s32[4]{0:T(128)} %region_ref.1) | copy-start | bytes 52
  8.3 0.7 %copy-start.8 = (s32[8]{0:T(128)S(1)}, s32[8]{0:T(128)}, u32[]{:S(2)}) copy-start(s32[8]{0:T(128)} %sources_ref.1) | copy-start | bytes 100

commit v3 on v2

--- a/solution.py
+++ b/solution.py
@@ -147,12 +147,13 @@
 
 
 def step_kernel(
-    state_ref, legendre_ref, weights_ref, region_ref, sources_ref, synth_ref, analysis_ref,
-    forward_ref, backward_ref, pick_ref, fourier_ref,
+    state_hbm, legendre_ref, weights_ref, region_ref, sources_ref, synth_hbm, analysis_hbm,
+    forward_hbm, backward_hbm, pick_hbm, fourier_hbm,
     out_ref, score_ref,
+    state_ref, synth_ref, analysis_ref, forward_ref, backward_ref, pick_ref, fourier_ref,
     leg, sent, held, flux, back_sent, back, score_buf, cross, crossed,
     pool0, pool1, pool2, pool3,
-    leg_sem, go_send, go_recv, ret_send, ret_recv, score_send, score_recv,
+    state_sem, table_sem, leg_sem, go_send, go_recv, ret_send, ret_recv, score_send, score_recv,
     pass_send, pass_recv, cross_send, cross_recv,
     *, scale, analysis_scale, waves_total,
 ):
@@ -171,13 +172,38 @@
     z_here = z_mate - half * 4
     points = synth_ref.shape[1] // 4
     degrees = state_ref.shape[1]
-    lat_count = weights_ref.shape[1]
+    lat_count = weights_ref.shape[0]
 
     loads = [
         pltpu.make_async_copy(legendre_ref.at[m], leg.at[m], leg_sem.at[m])
         for m in range(CHUNKS * PAIR)
     ]
-    for load in loads:
+    state_loads = [
+        pltpu.make_async_copy(
+            state_hbm.at[pl.ds(c * CHUNK_ROWS, CHUNK_ROWS)],
+            state_ref.at[pl.ds(c * CHUNK_ROWS, CHUNK_ROWS)],
+            state_sem.at[c],
+        )
+        for c in range(CHUNKS)
+    ]
+    table_pairs = [
+        (forward_hbm, forward_ref),
+        (fourier_hbm, fourier_ref),
+        (synth_hbm, synth_ref),
+        (analysis_hbm, analysis_ref),
+        (pick_hbm, pick_ref),
+        (backward_hbm, backward_ref),
+    ]
+    table_loads = [
+        pltpu.make_async_copy(pair[0], pair[1], table_sem.at[i])
+        for i, pair in enumerate(table_pairs)
+    ]
+    table_loads[0].start()
+    for c in range(CHUNKS):
+        state_loads[c].start()
+        for load in loads[c * PAIR : (c + 1) * PAIR]:
+            load.start()
+    for load in table_loads[1:]:
         load.start()
 
     barrier = pltpu.get_barrier_semaphore()
@@ -191,11 +217,6 @@
     @pl.when(inner)
     def _():
         pl.semaphore_signal(barrier, inc=1, device_id={"member": far_outer}, device_id_type=MESH)
-        pl.semaphore_wait(barrier, 7)
-
-    @pl.when(jnp.logical_not(inner))
-    def _():
-        pl.semaphore_wait(barrier, 6)
 
     def wave_copy(source, target, target_row, c, d, send_sem, recv_sem):
         to = (me + d) % WAVES
@@ -212,6 +233,9 @@
     go = []
     for c in range(CHUNKS):
         parts = []
+        state_loads[c].wait()
+        if c == 0:
+            table_loads[0].wait()
         for m in range(c * PAIR, (c + 1) * PAIR):
             loads[m].wait()
             parts.append(
@@ -229,6 +253,16 @@
             sent[w * OWNED_ROWS + c * PART_ROWS : w * OWNED_ROWS + (c + 1) * PART_ROWS] = ordered[
                 w * PART_ROWS : (w + 1) * PART_ROWS
             ]
+        if c == 0:
+
+            @pl.when(inner)
+            def _():
+                pl.semaphore_wait(barrier, 7)
+
+            @pl.when(jnp.logical_not(inner))
+            def _():
+                pl.semaphore_wait(barrier, 6)
+
         for d in (2, 1, 3):
             copy = wave_copy(sent, held, my_rows + c * PART_ROWS, c, d, go_send, go_recv)
             copy.start()
@@ -236,6 +270,8 @@
     mine = pl.ds(pl.multiple_of(my_rows, OWNED_ROWS), OWNED_ROWS)
     held[mine] = sent[mine]
 
+    for load in table_loads[1:]:
+        load.wait()
     low, high = region_ref[2], region_ref[3]
     lon = lax.broadcasted_iota(jnp.int32, (1, fourier_ref.shape[1]), 1)
     lon_inside = jnp.where((lon >= low) & (lon < high), 1.0, 0.0)
@@ -249,7 +285,7 @@
     gram_high = gram.astype(jnp.bfloat16)
     gram_low = (gram - gram_high.astype(jnp.float32)).astype(jnp.bfloat16)
     lat = lax.broadcasted_iota(jnp.int32, (1, lat_count), 1)
-    weights = weights_ref[...]
+    weights = weights_ref[...].reshape(1, lat_count)
     region_weights = jnp.where((lat >= region_ref[0]) & (lat < region_ref[1]), weights, 0.0)
     weight_sum = jnp.sum(region_weights, axis=1, keepdims=True) * (high - low).astype(jnp.float32)
 
@@ -422,8 +458,17 @@
     pick = np.zeros((2 * waves_total, 8 * waves_total))
     pick[np.arange(2 * waves_total), np.arange(2 * waves_total) * 4 + 3] = 1.0
     fourier = wave_table(waves_total, NLON).reshape(2 * waves_total, NLON).astype(jnp.bfloat16)
+    tables = [
+        jnp.asarray(np.stack([synth_high, synth_low])),
+        jnp.asarray(np.stack([synth_high.T, synth_low.T])),
+        jnp.asarray(forward),
+        jnp.asarray(backward),
+        jnp.asarray(pick.astype(jnp.bfloat16)),
+        jnp.asarray(fourier),
+    ]
     vmem = pl.BlockSpec(memory_space=pltpu.VMEM)
     smem = pl.BlockSpec(memory_space=pltpu.SMEM)
+    hbm = pl.BlockSpec(memory_space=pl.ANY)
     rows = waves_local * ROWS
     block = (rows, degrees)
     dma = pltpu.SemaphoreType.DMA
@@ -438,9 +483,11 @@
             jax.ShapeDtypeStruct(block, jnp.bfloat16),
             jax.ShapeDtypeStruct((8, 128), jnp.float32),
         ),
-        in_specs=[vmem, pl.BlockSpec(memory_space=pl.ANY), vmem, smem, smem] + [vmem] * 6,
+        in_specs=[hbm, hbm, vmem, smem, smem] + [hbm] * 6,
         out_specs=(vmem, vmem),
-        scratch_shapes=[
+        scratch_shapes=[pltpu.VMEM(block, jnp.float32)]
+        + [pltpu.VMEM(table.shape, table.dtype) for table in tables]
+        + [
             pltpu.VMEM(legendre.shape, jnp.bfloat16),
             pltpu.VMEM((rows, latitudes), jnp.bfloat16),
             pltpu.VMEM((rows, latitudes), jnp.bfloat16),
@@ -453,6 +500,8 @@
         ]
         + [pltpu.VMEM((4, CHUNK_ROWS, degrees), jnp.bfloat16)] * CHUNKS
         + [
+            dma((CHUNKS,)),
+            dma((len(tables),)),
             dma((waves_local,)),
             dma((WAVES - 1, CHUNKS)),
             dma((WAVES - 1, CHUNKS)),
@@ -466,20 +515,15 @@
             dma((CHUNKS,)),
         ],
         compiler_params=pltpu.CompilerParams(
-            collective_id=0, has_side_effects=True, vmem_limit_bytes=48 * 1024 * 1024
+            collective_id=0, has_side_effects=True, vmem_limit_bytes=56 * 1024 * 1024
         ),
     )(
         state.reshape(block),
         legendre,
-        lat_weights.reshape(1, latitudes),
+        lat_weights,
         region,
         sources,
-        jnp.asarray(np.stack([synth_high, synth_low])),
-        jnp.asarray(np.stack([synth_high.T, synth_low.T])),
-        jnp.asarray(forward),
-        jnp.asarray(backward),
-        jnp.asarray(pick.astype(jnp.bfloat16)),
-        jnp.asarray(fourier),
+        *tables,
     )
     return (cloned.astype(jnp.float32).reshape(state.shape), scores[0, :1])
 

time: 51.3 us -> 45.7 us (0.89)
  local copies, waits for them, and re-layouts: 8.84 us -> 1.19 us
  Pallas kernels: 40.4 us -> 41.8 us
  other arithmetic: 0.89 us -> 1.86 us
    unnamed x18 -> x0, local copies, waits for them, and re-layouts: 7.64 us -> none
    pallas_call x1, Pallas kernels: 40.4 us -> 41.8 us  [in_one_kernel(): pl.pallas_call(functools.partial(step_kernel, scale=(2.0 * waves_total) *...]
    reshape x1, other arithmetic: 0.89 us -> 1.86 us  [in_one_kernel(): return (cloned.astype(jnp.float32).reshape(state.shape), scores[0, :1])]
    reshape x1 -> x0, local copies, waits for them, and re-layouts: 0.69 us -> none  [in_one_kernel(): lat_weights.reshape(1, latitudes)]
    slice x1, local copies, waits for them, and re-layouts: 0.51 us -> 1.19 us  [in_one_kernel(): return (cloned.astype(jnp.float32).reshape(state.shape), scores[0, :1])]
where the time goes in v3:
time: 45.7 us; the launch traced here: 45.4 us
  Pallas kernels  41.8 us (91%)
  other arithmetic  1.86 us (4%)
  local copies, waits for them, and re-layouts  1.19 us (3%)
  between operations  0.64 us (1%)
    pallas_call x1, Pallas kernels, in_one_kernel(): pl.pallas_call(functools.partial(step_kernel, scale=(2.0 * waves_total) *...  41.8 us
    reshape x1, other arithmetic, in_one_kernel(): return (cloned.astype(jnp.float32).reshape(state.shape), scores[0, :1])  1.86 us
    slice x1, local copies, waits for them, and re-layouts, in_one_kernel(): return (cloned.astype(jnp.float32).reshape(state.shape), scores[0, :1])  1.19 us

profile of v3, /device:TPU:0, one launch (start us, length us, event | category | flops | bytes accessed | tf_op | source)
XLA Modules:
  0.0 45.4 jit_solution(8617671255634510899)
XLA Ops:
  0.6 41.8 %shard_map.122 = (bf16[256,640]{1,0:T(8,128)(2,1)}, f32[8,128]{1,0:T(8,128)}) custom-call(f32[256,640]{1,0:T(8,128)} %bitcast.4, bf16[8,640,640]{2,1,0:T(8,128)(2,1)} %legendre_ref.1, f32[640]{0:T(1024)} %weights_ref.1, s32[4]{0:T(128)} %region_ref.1, s32[8]{0:T(128)} %sources_ref.1, bf16[2,512,256]{2,1,0:T(8,128)(2,1)} %constant.12.clone.synth_hbm, ...), custom_call_target="tpu_custom_call" | custom-call | tf_op jit(solution)/shard_map/pallas_call | solution.py:475
  42.4 1.2 %slice.3 = f32[1,1]{1,0:T(1,128)} slice(f32[8,128]{1,0:T(8,128)} %get-tuple-element.5), slice={[0:1], [0:1]} | slice | bytes 8 | tf_op jit(solution)/shard_map/slice | solution.py:528
  43.6 1.9 %convert.1 = f32[1,8,32,640]{3,2,1,0:T(8,128)} convert(bf16[1,8,32,640]{3,2,1,0:T(8,128)(2,1)} %bitcast.5) | non-fusion elementwise | flops 163840 | bytes 983040 | tf_op jit(solution)/shard_map/reshape | solution.py:528

commit v4 on v1

--- a/solution.py
+++ b/solution.py
@@ -1,7 +1,11 @@
+import functools
+
 import jax
 import jax.numpy as jnp
 import numpy as np
 from jax import lax
+from jax.experimental import pallas as pl
+from jax.experimental.pallas import tpu as pltpu
 from jax.sharding import PartitionSpec as P
 
 NLON = 2560
@@ -110,9 +114,434 @@
     return (cloned, scores)
 
 
+MESH = pl.DeviceIdType.MESH
+WAVES = 4
+CHUNKS = 4
+STEPS = 8
+PAIR = 2
+ROWS = 32
+CHUNK_ROWS = PAIR * ROWS
+PART_ROWS = CHUNK_ROWS // WAVES
+OWNED_ROWS = CHUNKS * PART_ROWS
+
+
+def order_tables(levels):
+    held = levels // WAVES
+    forward = np.zeros((CHUNK_ROWS, CHUNK_ROWS))
+    backward = np.zeros((CHUNK_ROWS, CHUNK_ROWS))
+    for m in range(PAIR):
+        for c in range(2):
+            for f in range(2):
+                for k in range(levels):
+                    plain = ((m * 2 + c) * 2 + f) * levels + k
+                    owner = ((((k // held) * PAIR + m) * 2 + c) * 2 + f) * held + k % held
+                    crossed = ((((k // held) * PAIR + m) * 2 + (1 - c)) * 2 + f) * held + k % held
+                    forward[owner, plain] = 1.0
+                    backward[plain, crossed] = 1.0 - 2.0 * c
+    return forward.astype(jnp.bfloat16), backward.astype(jnp.bfloat16)
+
+
+def step_kernel(
+    state_hbm, legendre_ref, weights_ref, region_ref, sources_ref, table_hbm,
+    out_ref, score_ref,
+    state_ref, table_ref, synth_ref, analysis_ref, low_ref, low_sent, low_held,
+    chosen, leg, sent, held, flux, back_sent, back, cross, crossed,
+    *rest, scale, analysis_scale, waves_total, points,
+):
+    pools = rest[:STEPS]
+    (
+        state_sem, table_sem, leg_sem, go_send, go_recv, ret_send, ret_recv, score_send, score_recv,
+        pass_send, pass_recv, cross_send, cross_recv,
+    ) = rest[STEPS:]
+    me = lax.axis_index("wave")
+    slot = lax.axis_index("member")
+    z = slot // 2
+    x = slot % 2
+    half = z // 2
+    inner = z % 2 != half % 2
+    z_mate = (z + 1 - 2 * (z % 2)) * 2 + x
+    x_mate = z * 2 + 1 - x
+    far_inner = (2 - half) * 2 + x
+    far_outer = (3 - 3 * half) * 2 + x
+    here = slot - half * 4
+    z_here = z_mate - half * 4
+    degrees = state_ref.shape[1]
+    lat_count = weights_ref.shape[0]
+    f32 = jnp.float32
+    bf16 = jnp.bfloat16
+    low_level = ROWS // 4 - 1
+
+    loads = [
+        pltpu.make_async_copy(legendre_ref.at[m], leg.at[m], leg_sem.at[m]) for m in range(STEPS)
+    ]
+    state_loads = [
+        pltpu.make_async_copy(
+            state_hbm.at[pl.ds(c * CHUNK_ROWS, CHUNK_ROWS)],
+            state_ref.at[pl.ds(c * CHUNK_ROWS, CHUNK_ROWS)],
+            state_sem.at[c],
+        )
+        for c in range(CHUNKS)
+    ]
+    table_load = pltpu.make_async_copy(table_hbm, table_ref, table_sem)
+    for load in state_loads + [table_load] + loads:
+        load.start()
+
+    barrier = pltpu.get_barrier_semaphore()
+    for d in range(1, WAVES):
+        pl.semaphore_signal(
+            barrier, inc=1, device_id={"wave": (me + d) % WAVES}, device_id_type=MESH
+        )
+    for mate in (z_mate, x_mate, far_inner):
+        pl.semaphore_signal(barrier, inc=1, device_id={"member": mate}, device_id_type=MESH)
+
+    @pl.when(inner)
+    def _():
+        pl.semaphore_signal(barrier, inc=1, device_id={"member": far_outer}, device_id_type=MESH)
+
+    for c in range(CHUNKS):
+        state_loads[c].wait()
+        for m in range(c * PAIR, (c + 1) * PAIR):
+            pools[m][here] = state_ref[m * ROWS : (m + 1) * ROWS].astype(bf16)
+
+    @pl.when(inner)
+    def _():
+        pl.semaphore_wait(barrier, 7)
+
+    @pl.when(jnp.logical_not(inner))
+    def _():
+        pl.semaphore_wait(barrier, 6)
+
+    def member_copy(source, target, to, send_sem, recv_sem):
+        return pltpu.make_async_remote_copy(
+            src_ref=source, dst_ref=target, send_sem=send_sem, recv_sem=recv_sem,
+            device_id={"member": to}, device_id_type=MESH,
+        )
+
+    def pass_copy(c, kind):
+        block = pools[c].at[z_here if kind == 2 else here]
+        return member_copy(
+            block, block, z_mate if kind == 0 else x_mate, pass_send.at[kind, c], pass_recv.at[kind, c]
+        )
+
+    def cross_copy(c, far):
+        return member_copy(
+            cross.at[c, far],
+            crossed.at[c],
+            far_outer if far else far_inner,
+            cross_send.at[far, c],
+            cross_recv.at[c],
+        )
+
+    def half_index(member_slot):
+        return jnp.clip(sources_ref[member_slot] - half * 4, 0, 3)
+
+    inner_pick = half_index(far_inner)
+    outer_pick = half_index(far_outer)
+    origin = sources_ref[slot] - half * 4
+    near = (origin >= 0) & (origin < 4)
+    choice = jnp.clip(origin, 0, 3)
+
+    for c in range(STEPS):
+        pass_copy(c, 0).start()
+        if c < 2:
+            pass_copy(c, 1).start()
+
+    def forward_pass(c):
+        pass_copy(c, 0).wait_recv()
+        pass_copy(c, 2).start()
+        if c + 2 < STEPS:
+            pass_copy(c + 2, 1).start()
+
+    def send_across(c):
+        pass_copy(c, 1).wait_recv()
+        pass_copy(c, 2).wait_recv()
+
+        @pl.when(inner)
+        def _():
+            cross[c, 1] = pools[c][outer_pick]
+            cross_copy(c, 1).start()
+            cross[c, 0] = pools[c][inner_pick]
+            cross_copy(c, 0).start()
+
+    def lowest_coef(m):
+        loads[m].wait()
+        coef = jnp.dot(
+            state_ref[m * ROWS : (m + 1) * ROWS].astype(bf16), leg[m], preferred_element_type=f32
+        )
+        for c in range(2):
+            row = c * (ROWS // 2) + ROWS // 4 + low_level
+            low_ref[m * 2 + c : m * 2 + c + 1] = coef[row : row + 1]
+
+    def wave_copy(source, target, target_row, c, d, send_sem, recv_sem):
+        to = (me + d) % WAVES
+        return pltpu.make_async_remote_copy(
+            src_ref=source.at[pl.ds(pl.multiple_of(to * OWNED_ROWS + c * PART_ROWS, PART_ROWS), PART_ROWS)],
+            dst_ref=target.at[pl.ds(pl.multiple_of(target_row, PART_ROWS), PART_ROWS)],
+            send_sem=send_sem.at[d - 1, c],
+            recv_sem=recv_sem.at[d - 1, c],
+            device_id={"wave": to},
+            device_id_type=MESH,
+        )
+
+    def low_copy(d):
+        return pltpu.make_async_remote_copy(
+            src_ref=low_sent,
+            dst_ref=low_held.at[pl.ds(pl.multiple_of(me * 16, 16), 16)],
+            send_sem=score_send.at[d - 1],
+            recv_sem=score_recv.at[d - 1],
+            device_id={"wave": (me + d) % WAVES},
+            device_id_type=MESH,
+        )
+
+    my_rows = me * OWNED_ROWS
+    mine = pl.ds(pl.multiple_of(my_rows, OWNED_ROWS), OWNED_ROWS)
+    columns = fourier_columns = table_ref.shape[1] - 4 * 128
+    go = []
+    coef_parts = []
+
+    def take_source(c):
+        cross_copy(c, 0).wait_recv()
+        block = jnp.where(near, pools[c][choice], crossed[c])
+        chosen[c * ROWS : (c + 1) * ROWS] = block
+        coef_parts.append(jnp.dot(block, leg[c], preferred_element_type=f32))
+        if c % PAIR != PAIR - 1:
+            return
+        pair = c // PAIR
+        coef = jnp.concatenate(coef_parts[-PAIR:], axis=0).astype(bf16)
+        forward = table_ref[:, columns + 256 : columns + 256 + CHUNK_ROWS]
+        ordered = jnp.dot(forward, coef, preferred_element_type=f32).astype(bf16)
+        for w in range(WAVES):
+            first = w * OWNED_ROWS + pair * PART_ROWS
+            sent[first : first + PART_ROWS] = ordered[w * PART_ROWS : (w + 1) * PART_ROWS]
+        for d in (2, 1, 3):
+            copy = wave_copy(sent, held, my_rows + pair * PART_ROWS, pair, d, go_send, go_recv)
+            copy.start()
+            go.append(copy)
+
+    table_load.wait()
+    coef_rows = 4 * 2 * waves_total
+    owner_of = lax.broadcasted_iota(jnp.int32, (2 * waves_total, coef_rows), 0)
+    column = lax.broadcasted_iota(jnp.int32, (2 * waves_total, coef_rows), 1)
+    widen = jnp.where(column // 4 == owner_of, 1.0, 0.0).astype(bf16)
+    tall_owner = lax.broadcasted_iota(jnp.int32, (coef_rows, 2 * waves_total), 1)
+    tall_row = lax.broadcasted_iota(jnp.int32, (coef_rows, 2 * waves_total), 0)
+    lengthen = jnp.where(tall_row // 4 == tall_owner, 1.0, 0.0).astype(bf16)
+    synth_column = lax.broadcasted_iota(jnp.int32, (points, coef_rows), 1) % 4
+    analysis_row = lax.broadcasted_iota(jnp.int32, (coef_rows, points), 0) % 4
+    for part in range(2):
+        waves = table_ref[:, columns + part * 128 : columns + part * 128 + points]
+        wide = lax.dot_general(
+            waves, widen, (((0,), (0,)), ((), ())), preferred_element_type=f32
+        )
+        tall = jnp.dot(lengthen, waves, preferred_element_type=f32)
+        for k in range(2):
+            for f in range(2):
+                at = slice((k * 2 + f) * points, (k * 2 + f + 1) * points)
+                synth_ref[part, at] = jnp.where(synth_column == f * 2 + k, wide, 0.0).astype(bf16)
+                analysis_ref[part, :, at] = jnp.where(
+                    analysis_row == f * 2 + k, tall, 0.0
+                ).astype(bf16)
+
+    low, high = region_ref[2], region_ref[3]
+    lon = lax.broadcasted_iota(jnp.int32, (1, fourier_columns), 1)
+    lon_inside = jnp.where((lon >= low) & (lon < high), 1.0, 0.0)
+    fourier = table_ref[:, :fourier_columns]
+    gram = lax.dot_general(
+        (fourier.astype(f32) * lon_inside).astype(bf16),
+        fourier,
+        (((1,), (1,)), ((), ())),
+        preferred_element_type=f32,
+    )
+    gram_high = gram.astype(bf16)
+    gram_low = (gram - gram_high.astype(f32)).astype(bf16)
+    lat = lax.broadcasted_iota(jnp.int32, (1, lat_count), 1)
+    weights = weights_ref[...].reshape(1, lat_count)
+    region_weights = jnp.where((lat >= region_ref[0]) & (lat < region_ref[1]), weights, 0.0)
+    weight_sum = jnp.sum(region_weights, axis=1, keepdims=True) * (high - low).astype(f32)
+
+    for t in range(STEPS + 4):
+        if t < STEPS:
+            forward_pass(t)
+            lowest_coef(t)
+        if t == STEPS - 1:
+            low_sent[...] = low_ref[...].astype(bf16)
+            low_held[pl.ds(pl.multiple_of(me * 16, 16), 16)] = low_sent[...]
+            for d in range(1, WAVES):
+                low_copy(d).start()
+        if 1 <= t <= STEPS:
+            send_across(t - 1)
+        if t >= 4:
+            take_source(t - 4)
+    held[mine] = sent[mine]
+
+    for copy in go:
+        copy.wait_recv()
+
+    coefs = held[...]
+    scaled = weights * (scale * scale)
+    for k in range(2):
+        rows = slice(k * 2 * points, (k + 1) * 2 * points)
+        grid = jnp.dot(synth_ref[0, rows], coefs, preferred_element_type=f32) + jnp.dot(
+            synth_ref[1, rows], coefs, preferred_element_type=f32
+        )
+        wind = grid[:points]
+        weighted = wind * scaled
+        flux[k * 2 * points : (k * 2 + 1) * points] = (0.5 * weighted * wind).astype(bf16)
+        flux[(k * 2 + 1) * points : (k * 2 + 2) * points] = (weighted * grid[points:]).astype(bf16)
+    fluxes = flux[...]
+    back_sent[...] = (
+        analysis_scale
+        * (
+            jnp.dot(analysis_ref[0], fluxes, preferred_element_type=f32)
+            + jnp.dot(analysis_ref[1], fluxes, preferred_element_type=f32)
+        )
+    ).astype(bf16)
+    ret = []
+    for c in range(CHUNKS):
+        for d in (2, 1, 3):
+            copy = wave_copy(back_sent, back, my_rows + c * PART_ROWS, c, d, ret_send, ret_recv)
+            copy.start()
+            ret.append(copy)
+    back[mine] = back_sent[mine]
+
+    for d in range(1, WAVES):
+        low_copy(d).wait()
+    lowest = low_held[...]
+    spread = jnp.dot(gram_high, lowest, preferred_element_type=f32) + jnp.dot(
+        gram_low, lowest, preferred_element_type=f32
+    )
+    squares = jnp.sum(lowest.astype(f32) * spread, axis=0, keepdims=True) * (
+        region_weights * (scale * scale)
+    )
+    score = jnp.sum(squares, axis=1, keepdims=True) / weight_sum
+    score_ref[...] = jnp.broadcast_to(score, score_ref.shape)
+
+    degree = lax.broadcasted_iota(jnp.int32, (1, degrees), 1).astype(f32)
+    keep = 1.0 / (1.0 + ((degree + 1.0) / degrees) ** 2)
+    backward = table_ref[:, columns + 384 : columns + 384 + CHUNK_ROWS]
+    for c in range(CHUNKS):
+        for copy in ret[c * (WAVES - 1) : (c + 1) * (WAVES - 1)]:
+            copy.wait_recv()
+        arrived = jnp.concatenate(
+            [
+                back[w * OWNED_ROWS + c * PART_ROWS : w * OWNED_ROWS + (c + 1) * PART_ROWS]
+                for w in range(WAVES)
+            ],
+            axis=0,
+        )
+        plain = jnp.dot(backward, arrived, preferred_element_type=f32).astype(bf16)
+        for i in range(PAIR):
+            m = c * PAIR + i
+            tendency = lax.dot_general(
+                plain[i * ROWS : (i + 1) * ROWS],
+                leg[m],
+                (((1,), (1,)), ((), ())),
+                preferred_element_type=f32,
+            )
+            wave_id = (me * STEPS + m).astype(f32)
+            advection = wave_id * (advect_rate / waves_total)
+            source = chosen[m * ROWS : (m + 1) * ROWS].astype(f32)
+            out_ref[m * ROWS : (m + 1) * ROWS] = (source + advection * tendency) * keep
+
+    for copy in go + ret:
+        copy.wait_send()
+    for c in range(STEPS):
+        for kind in range(3):
+            pass_copy(c, kind).wait_send()
+
+    @pl.when(inner)
+    def _():
+        for c in range(STEPS):
+            for far in range(2):
+                cross_copy(c, far).wait_send()
+
+
+def in_one_kernel(state, legendre, lat_weights, region, sources):
+    waves_local, degrees, latitudes = legendre.shape
+    waves_total = waves_local * WAVES
+    points = quadrature_points(waves_total)
+    table_high, table_low = split_table(wave_table(waves_total, points))
+    fourier = wave_table(waves_total, NLON).astype(jnp.bfloat16)
+    forward, backward = order_tables(state.shape[2] // 4)
+    unused = np.zeros((CHUNK_ROWS, 128 - CHUNK_ROWS), jnp.bfloat16)
+    flat = [t.reshape(2 * waves_total, -1) for t in (fourier, table_high, table_low)]
+    table = np.concatenate(flat + [forward, unused, backward, unused], axis=1)
+    vmem = pl.BlockSpec(memory_space=pltpu.VMEM)
+    smem = pl.BlockSpec(memory_space=pltpu.SMEM)
+    hbm = pl.BlockSpec(memory_space=pl.ANY)
+    rows = waves_local * ROWS
+    block = (rows, degrees)
+    grid_rows = (rows, latitudes)
+    dma = pltpu.SemaphoreType.DMA
+    bf16 = jnp.bfloat16
+    stepped, scores = pl.pallas_call(
+        functools.partial(
+            step_kernel,
+            scale=(2.0 * waves_total) ** -0.5,
+            analysis_scale=NLON**-0.5 * (NLON / points),
+            waves_total=waves_total,
+            points=points,
+        ),
+        out_shape=(
+            jax.ShapeDtypeStruct(block, jnp.float32),
+            jax.ShapeDtypeStruct((8, 128), jnp.float32),
+        ),
+        in_specs=[hbm, hbm, vmem, smem, smem, hbm],
+        out_specs=(vmem, vmem),
+        scratch_shapes=[
+            pltpu.VMEM(block, jnp.float32),
+            pltpu.VMEM(table.shape, bf16),
+            pltpu.VMEM((2, 4 * points, 8 * waves_total), bf16),
+            pltpu.VMEM((2, 8 * waves_total, 4 * points), bf16),
+            pltpu.VMEM((2 * waves_local, latitudes), jnp.float32),
+            pltpu.VMEM((2 * waves_local, latitudes), bf16),
+            pltpu.VMEM((2 * waves_total, latitudes), bf16),
+            pltpu.VMEM(block, bf16),
+            pltpu.VMEM(legendre.shape, bf16),
+            pltpu.VMEM(grid_rows, bf16),
+            pltpu.VMEM(grid_rows, bf16),
+            pltpu.VMEM((4 * points, latitudes), bf16),
+            pltpu.VMEM(grid_rows, bf16),
+            pltpu.VMEM(grid_rows, bf16),
+            pltpu.VMEM((STEPS, 2, ROWS, degrees), bf16),
+            pltpu.VMEM((STEPS, ROWS, degrees), bf16),
+        ]
+        + [pltpu.VMEM((4, ROWS, degrees), bf16)] * STEPS
+        + [
+            dma((CHUNKS,)),
+            dma,
+            dma((STEPS,)),
+            dma((WAVES - 1, CHUNKS)),
+            dma((WAVES - 1, CHUNKS)),
+            dma((WAVES - 1, CHUNKS)),
+            dma((WAVES - 1, CHUNKS)),
+            dma((WAVES - 1,)),
+            dma((WAVES - 1,)),
+            dma((3, STEPS)),
+            dma((3, STEPS)),
+            dma((2, STEPS)),
+            dma((STEPS,)),
+        ],
+        compiler_params=pltpu.CompilerParams(
+            collective_id=0, has_side_effects=True, vmem_limit_bytes=48 * 1024 * 1024
+        ),
+    )(state.reshape(block), legendre, lat_weights, region, sources, jnp.asarray(table))
+    return (stepped.reshape(state.shape), scores[0, :1])
+
+
 def solution(mesh):
     in_specs = (P("member", "wave", None, None), P("wave", None, None), P(), P(), P())
     out_specs = (P("member", "wave", None, None), P("member"))
-    return jax.shard_map(
-        on_device, mesh=mesh, in_specs=in_specs, out_specs=out_specs, check_vma=False
-    )
+
+    def run(state, legendre, lat_weights, region, sources):
+        shape = (state.shape[1] // mesh.shape["wave"], state.shape[2], state.shape[3], legendre.shape[2])
+        fits = mesh.shape["wave"] == 4 and mesh.shape["member"] == 8 and shape == (8, 32, 640, 640)
+        return jax.shard_map(
+            in_one_kernel if fits else on_device,
+            mesh=mesh,
+            in_specs=in_specs,
+            out_specs=out_specs,
+            check_vma=False,
+        )(state, legendre, lat_weights, region, sources)
+
+    return run

time: 124 us -> 47 us (0.38)
  waiting for transfers between devices: 53.7 us -> 0 us
  Pallas kernels: 0 us -> 40.7 us
  between operations: 20.1 us -> 0.65 us
  matrix products: 11.8 us -> 0 us
  local copies, waits for them, and re-layouts: 17.2 us -> 5.42 us
  starting transfers between devices: 7.75 us -> 0 us
  other arithmetic: 7.19 us -> 0 us
  blocking collectives: 6.27 us -> 0 us
    pallas_call x0 -> x1, Pallas kernels: none -> 40.7 us  [in_one_kernel(): pl.pallas_call(functools.partial(step_kernel, scale=(2.0 * waves_total) *...]
    all_gather x1 -> x0, waiting for transfers between devices: 40.1 us -> none  [on_device(): lax.all_gather(stepped.astype(jnp.bfloat16), 'member', axis=0, tiled=True)]
    all_to_all x2 -> x0, waiting for transfers between devices: 13.6 us -> none  [the longest x1 8.73 us: on_device(): lax.all_to_all(flux_coef, 'wave', split_axis=0, concat_axis=3, tiled=True)]
    dot_general x7 -> x0, matrix products: 11.8 us -> none  [the longest x1 4.95 us: on_device(): jnp.einsum('mckl,mnl->mckn', lax.all_to_all(flux_coef, 'wave', split_axis...]
    all_to_all x2 -> x0, starting transfers between devices: 7.71 us -> none  [the longest x1 4.24 us: on_device(): lax.all_to_all(fourier_coef, 'wave', split_axis=3, concat_axis=0, tiled=T...]
    psum x1 -> x0, blocking collectives: 6.27 us -> none  [on_device(): region_total = lax.psum(region_part, 'wave')]
    all_to_all x3 -> x0, local copies, waits for them, and re-layouts: 5.42 us -> none  [the longest x1 4.69 us: on_device(): lax.all_to_all(fourier_coef, 'wave', split_axis=3, concat_axis=0, tiled=T...]
    reshape x1 -> x0, local copies, waits for them, and re-layouts: 3.3 us -> none  [on_device(): fourier_coef.astype(jnp.bfloat16)]
  transfers between devices with their start and end apart: 3 -> 0, of which waited for: 3 -> 0; matrix products, arithmetic and copies ran while one was open for 5% -> 0% of each run, Pallas kernels for 0% -> 0%
where the time goes in v4:
time: 47 us; the launch traced here: 46.8 us
  Pallas kernels  40.7 us (87%)
  local copies, waits for them, and re-layouts  5.42 us (12%)
  between operations  0.65 us (1%)
    pallas_call x1, Pallas kernels, in_one_kernel(): pl.pallas_call(functools.partial(step_kernel, scale=(2.0 * waves_total) *...  40.7 us
    unnamed x11, local copies, waits for them, and re-layouts  4.91 us

profile of v4, /device:TPU:0, one launch (start us, length us, event | category | flops | bytes accessed | tf_op | source)
XLA Modules:
  0.0 46.8 jit_solution(5358338663473149263)
XLA Ops:
  0.6 0.0 copy-start
  0.6 1.1 %copy-done = f32[1,8,32,640]{3,2,1,0:T(8,128)S(1)} copy-done((f32[1,8,32,640]{3,2,1,0:T(8,128)S(1)}, f32[1,8,32,640]{3,2,1,0:T(8,128)}, u32[]{:S(2)}) %copy-start) | copy-done | bytes 655384
  1.7 0.0 copy-start.1
  1.7 1.0 %copy-done.1 = bf16[64,3072]{1,0:T(8,128)(2,1)S(1)} copy-done((bf16[64,3072]{1,0:T(8,128)(2,1)S(1)}, bf16[64,3072]{1,0:T(8,128)(2,1)}, u32[]{:S(2)}) %copy-start.1) | copy-done | bytes 393240
  2.7 0.0 copy-start.2
  2.7 0.7 %copy-done.2 = f32[640]{0:T(1024)S(1)} copy-done((f32[640]{0:T(1024)S(1)}, f32[640]{0:T(1024)}, u32[]{:S(2)}) %copy-start.2) | copy-done | bytes 2584
  3.4 0.0 copy-start.3
  3.4 0.7 %copy-done.3 = s32[4]{0:T(128)S(1)} copy-done((s32[4]{0:T(128)S(1)}, s32[4]{0:T(128)}, u32[]{:S(2)}) %copy-start.3) | copy-done | bytes 40
  4.1 0.0 copy-start.4
  4.1 0.7 %copy-done.4 = s32[8]{0:T(128)S(1)} copy-done((s32[8]{0:T(128)S(1)}, s32[8]{0:T(128)}, u32[]{:S(2)}) %copy-start.4) | copy-done | bytes 56
  4.7 40.7 %shard_map.77 = (f32[256,640]{1,0:T(8,128)S(1)}, f32[8,128]{1,0:T(8,128)S(1)}) custom-call(f32[256,640]{1,0:T(8,128)S(1)} %bitcast.3, bf16[8,640,640]{2,1,0:T(8,128)(2,1)} %legendre_ref.1, f32[640]{0:T(1024)S(1)} %copy-done.2, s32[4]{0:T(128)S(1)} %copy-done.3, s32[8]{0:T(128)S(1)} %copy-done.4, bf16[64,3072]{1,0:T(8,128)(2,1)S(1)} %copy-done.1), custom_call_target="tpu_custom_call" | custom-call | tf_op jit(solution)/shard_map/pallas_call | solution.py:477
  45.4 0.5 %slice.3 = f32[1,1]{1,0:T(1,128)} slice(f32[8,128]{1,0:T(8,128)S(1)} %get-tuple-element.5), slice={[0:1], [0:1]} | slice | bytes 8 | tf_op jit(solution)/shard_map/slice | solution.py:529
  45.9 0.8 %copy.9 = f32[1,8,32,640]{3,2,1,0:T(8,128)} copy(f32[1,8,32,640]{3,2,1,0:T(8,128)S(1)} %bitcast.4) | data formatting | bytes 1310720
Async XLA Ops:
  0.6 1.1 %copy-start = (f32[1,8,32,640]{3,2,1,0:T(8,128)S(1)}, f32[1,8,32,640]{3,2,1,0:T(8,128)}, u32[]{:S(2)}) copy-start(f32[1,8,32,640]{3,2,1,0:T(8,128)} %param.6) | copy-start | bytes 1966084
  1.7 1.0 %copy-start.1 = (bf16[64,3072]{1,0:T(8,128)(2,1)S(1)}, bf16[64,3072]{1,0:T(8,128)(2,1)}, u32[]{:S(2)}) copy-start(bf16[64,3072]{1,0:T(8,128)(2,1)} %constant.2.clone.table_hbm) | copy-start | bytes 1179652
  2.7 0.7 %copy-start.2 = (f32[640]{0:T(1024)S(1)}, f32[640]{0:T(1024)}, u32[]{:S(2)}) copy-start(f32[640]{0:T(1024)} %weights_ref.1) | copy-start | bytes 7684
  3.4 0.7 %copy-start.3 = (s32[4]{0:T(128)S(1)}, s32[4]{0:T(128)}, u32[]{:S(2)}) copy-start(s32[4]{0:T(128)} %region_ref.1) | copy-start | bytes 52
  4.1 0.7 %copy-start.4 = (s32[8]{0:T(128)S(1)}, s32[8]{0:T(128)}, u32[]{:S(2)}) copy-start(s32[8]{0:T(128)} %sources_ref.1) | copy-start | bytes 100

commit v5 on v4

--- a/solution.py
+++ b/solution.py
@@ -116,43 +116,42 @@
 
 MESH = pl.DeviceIdType.MESH
 WAVES = 4
-CHUNKS = 4
-STEPS = 8
-PAIR = 2
+CHUNKS = 2
+PAIR = 4
 ROWS = 32
-CHUNK_ROWS = PAIR * ROWS
+SET_ROWS = ROWS // 2
+LOCAL_WAVES = CHUNKS * PAIR
+CHUNK_ROWS = PAIR * SET_ROWS
 PART_ROWS = CHUNK_ROWS // WAVES
 OWNED_ROWS = CHUNKS * PART_ROWS
-
-
-def order_tables(levels):
-    held = levels // WAVES
+STEPS = 4
+
+
+def order_tables():
     forward = np.zeros((CHUNK_ROWS, CHUNK_ROWS))
     backward = np.zeros((CHUNK_ROWS, CHUNK_ROWS))
     for m in range(PAIR):
         for c in range(2):
             for f in range(2):
-                for k in range(levels):
-                    plain = ((m * 2 + c) * 2 + f) * levels + k
-                    owner = ((((k // held) * PAIR + m) * 2 + c) * 2 + f) * held + k % held
-                    crossed = ((((k // held) * PAIR + m) * 2 + (1 - c)) * 2 + f) * held + k % held
-                    forward[owner, plain] = 1.0
-                    backward[plain, crossed] = 1.0 - 2.0 * c
+                for k in range(WAVES):
+                    plain = ((m * 2 + c) * 2 + f) * WAVES + k
+                    forward[((k * PAIR + m) * 2 + c) * 2 + f, plain] = 1.0
+                    backward[plain, ((k * PAIR + m) * 2 + 1 - c) * 2 + f] = 1.0 - 2.0 * c
     return forward.astype(jnp.bfloat16), backward.astype(jnp.bfloat16)
 
 
 def step_kernel(
     state_hbm, legendre_ref, weights_ref, region_ref, sources_ref, table_hbm,
     out_ref, score_ref,
-    state_ref, table_ref, synth_ref, analysis_ref, low_ref, low_sent, low_held,
+    state_ref, set_ref, table_ref, synth_ref, analysis_ref, low_ref, low_sent, low_held,
     chosen, leg, sent, held, flux, back_sent, back, cross, crossed,
     *rest, scale, analysis_scale, waves_total, points,
 ):
-    pools = rest[:STEPS]
+    pools = rest[: 2 * STEPS]
     (
         state_sem, table_sem, leg_sem, go_send, go_recv, ret_send, ret_recv, score_send, score_recv,
         pass_send, pass_recv, cross_send, cross_recv,
-    ) = rest[STEPS:]
+    ) = rest[2 * STEPS :]
     me = lax.axis_index("wave")
     slot = lax.axis_index("member")
     z = slot // 2
@@ -169,15 +168,15 @@
     lat_count = weights_ref.shape[0]
     f32 = jnp.float32
     bf16 = jnp.bfloat16
-    low_level = ROWS // 4 - 1
+    levels = ROWS // 4
 
     loads = [
-        pltpu.make_async_copy(legendre_ref.at[m], leg.at[m], leg_sem.at[m]) for m in range(STEPS)
+        pltpu.make_async_copy(legendre_ref.at[m], leg.at[m], leg_sem.at[m]) for m in range(LOCAL_WAVES)
     ]
     state_loads = [
         pltpu.make_async_copy(
-            state_hbm.at[pl.ds(c * CHUNK_ROWS, CHUNK_ROWS)],
-            state_ref.at[pl.ds(c * CHUNK_ROWS, CHUNK_ROWS)],
+            state_hbm.at[pl.ds(c * PAIR * ROWS, PAIR * ROWS)],
+            state_ref.at[pl.ds(c * PAIR * ROWS, PAIR * ROWS)],
             state_sem.at[c],
         )
         for c in range(CHUNKS)
@@ -201,7 +200,13 @@
     for c in range(CHUNKS):
         state_loads[c].wait()
         for m in range(c * PAIR, (c + 1) * PAIR):
-            pools[m][here] = state_ref[m * ROWS : (m + 1) * ROWS].astype(bf16)
+            for group in range(4):
+                for early in range(2):
+                    first = m * SET_ROWS + group * WAVES
+                    source = m * ROWS + group * levels + (1 - early) * WAVES
+                    set_ref[1 - early, first : first + WAVES] = state_ref[source : source + WAVES]
+        for g in range(c * 2, c * 2 + 2):
+            pools[g][here] = set_ref[0, g * ROWS : (g + 1) * ROWS].astype(bf16)
 
     @pl.when(inner)
     def _():
@@ -241,15 +246,18 @@
     near = (origin >= 0) & (origin < 4)
     choice = jnp.clip(origin, 0, 3)
 
+    def begin_pass(c):
+        pass_copy(c, 0).start()
+        if c % STEPS < 2:
+            pass_copy(c, 1).start()
+
     for c in range(STEPS):
-        pass_copy(c, 0).start()
-        if c < 2:
-            pass_copy(c, 1).start()
+        begin_pass(c)
 
     def forward_pass(c):
         pass_copy(c, 0).wait_recv()
         pass_copy(c, 2).start()
-        if c + 2 < STEPS:
+        if c % STEPS + 2 < STEPS:
             pass_copy(c + 2, 1).start()
 
     def send_across(c):
@@ -263,22 +271,13 @@
             cross[c, 0] = pools[c][inner_pick]
             cross_copy(c, 0).start()
 
-    def lowest_coef(m):
-        loads[m].wait()
-        coef = jnp.dot(
-            state_ref[m * ROWS : (m + 1) * ROWS].astype(bf16), leg[m], preferred_element_type=f32
-        )
-        for c in range(2):
-            row = c * (ROWS // 2) + ROWS // 4 + low_level
-            low_ref[m * 2 + c : m * 2 + c + 1] = coef[row : row + 1]
-
-    def wave_copy(source, target, target_row, c, d, send_sem, recv_sem):
+    def wave_copy(source, target, h, c, d, send_sem, recv_sem):
         to = (me + d) % WAVES
         return pltpu.make_async_remote_copy(
-            src_ref=source.at[pl.ds(pl.multiple_of(to * OWNED_ROWS + c * PART_ROWS, PART_ROWS), PART_ROWS)],
-            dst_ref=target.at[pl.ds(pl.multiple_of(target_row, PART_ROWS), PART_ROWS)],
-            send_sem=send_sem.at[d - 1, c],
-            recv_sem=recv_sem.at[d - 1, c],
+            src_ref=source.at[h, pl.ds(pl.multiple_of(to * OWNED_ROWS + c * PART_ROWS, PART_ROWS), PART_ROWS)],
+            dst_ref=target.at[h, pl.ds(pl.multiple_of(me * OWNED_ROWS + c * PART_ROWS, PART_ROWS), PART_ROWS)],
+            send_sem=send_sem.at[h, d - 1, c],
+            recv_sem=recv_sem.at[h, d - 1, c],
             device_id={"wave": to},
             device_id_type=MESH,
         )
@@ -296,51 +295,77 @@
     my_rows = me * OWNED_ROWS
     mine = pl.ds(pl.multiple_of(my_rows, OWNED_ROWS), OWNED_ROWS)
     columns = fourier_columns = table_ref.shape[1] - 4 * 128
-    go = []
-    coef_parts = []
-
-    def take_source(c):
-        cross_copy(c, 0).wait_recv()
-        block = jnp.where(near, pools[c][choice], crossed[c])
-        chosen[c * ROWS : (c + 1) * ROWS] = block
-        coef_parts.append(jnp.dot(block, leg[c], preferred_element_type=f32))
-        if c % PAIR != PAIR - 1:
-            return
-        pair = c // PAIR
-        coef = jnp.concatenate(coef_parts[-PAIR:], axis=0).astype(bf16)
+
+    def go_copy(h, c, d):
+        return wave_copy(sent, held, h, c, d, go_send, go_recv)
+
+    def ret_copy(h, c, d):
+        return wave_copy(back_sent, back, h, c, d, ret_send, ret_recv)
+
+    def transform(h, c):
+        parts = []
+        for m in range(c * PAIR, (c + 1) * PAIR):
+            rows = slice(m * SET_ROWS, (m + 1) * SET_ROWS)
+            if h == 1:
+                loads[m].wait()
+                block = set_ref[1, rows].astype(bf16)
+            else:
+                block = chosen[rows]
+            part = jnp.dot(block, leg[m], preferred_element_type=f32)
+            parts.append(part)
+            if h == 1:
+                for real in range(2):
+                    row = (real + 1) * (SET_ROWS // 2) - 1
+                    low_ref[m * 2 + real : m * 2 + real + 1] = part[row : row + 1]
+        coef = jnp.concatenate(parts, axis=0).astype(bf16)
         forward = table_ref[:, columns + 256 : columns + 256 + CHUNK_ROWS]
         ordered = jnp.dot(forward, coef, preferred_element_type=f32).astype(bf16)
         for w in range(WAVES):
-            first = w * OWNED_ROWS + pair * PART_ROWS
-            sent[first : first + PART_ROWS] = ordered[w * PART_ROWS : (w + 1) * PART_ROWS]
+            first = w * OWNED_ROWS + c * PART_ROWS
+            sent[h, first : first + PART_ROWS] = ordered[w * PART_ROWS : (w + 1) * PART_ROWS]
         for d in (2, 1, 3):
-            copy = wave_copy(sent, held, my_rows + pair * PART_ROWS, pair, d, go_send, go_recv)
-            copy.start()
-            go.append(copy)
+            go_copy(h, c, d).start()
+
+    def take_source(g):
+        cross_copy(g, 0).wait_recv()
+        return jnp.where(near, pools[g][choice], crossed[g])
 
     table_load.wait()
-    coef_rows = 4 * 2 * waves_total
+    transform(1, 0)
+    forward_pass(0)
+    transform(1, 1)
+    low_sent[...] = low_ref[...].astype(bf16)
+    low_held[pl.ds(pl.multiple_of(me * 16, 16), 16)] = low_sent[...]
+    for d in range(1, WAVES):
+        low_copy(d).start()
+    held[1, mine] = sent[1, mine]
+    forward_pass(1)
+    forward_pass(2)
+    send_across(0)
+
+    coef_rows = 4 * waves_total
     owner_of = lax.broadcasted_iota(jnp.int32, (2 * waves_total, coef_rows), 0)
     column = lax.broadcasted_iota(jnp.int32, (2 * waves_total, coef_rows), 1)
-    widen = jnp.where(column // 4 == owner_of, 1.0, 0.0).astype(bf16)
+    widen = jnp.where(column // 2 == owner_of, 1.0, 0.0).astype(bf16)
     tall_owner = lax.broadcasted_iota(jnp.int32, (coef_rows, 2 * waves_total), 1)
     tall_row = lax.broadcasted_iota(jnp.int32, (coef_rows, 2 * waves_total), 0)
-    lengthen = jnp.where(tall_row // 4 == tall_owner, 1.0, 0.0).astype(bf16)
-    synth_column = lax.broadcasted_iota(jnp.int32, (points, coef_rows), 1) % 4
-    analysis_row = lax.broadcasted_iota(jnp.int32, (coef_rows, points), 0) % 4
+    lengthen = jnp.where(tall_row // 2 == tall_owner, 1.0, 0.0).astype(bf16)
+    synth_column = lax.broadcasted_iota(jnp.int32, (points, coef_rows), 1) % 2
+    analysis_row = lax.broadcasted_iota(jnp.int32, (coef_rows, points), 0) % 2
     for part in range(2):
         waves = table_ref[:, columns + part * 128 : columns + part * 128 + points]
         wide = lax.dot_general(
             waves, widen, (((0,), (0,)), ((), ())), preferred_element_type=f32
         )
         tall = jnp.dot(lengthen, waves, preferred_element_type=f32)
-        for k in range(2):
-            for f in range(2):
-                at = slice((k * 2 + f) * points, (k * 2 + f + 1) * points)
-                synth_ref[part, at] = jnp.where(synth_column == f * 2 + k, wide, 0.0).astype(bf16)
-                analysis_ref[part, :, at] = jnp.where(
-                    analysis_row == f * 2 + k, tall, 0.0
-                ).astype(bf16)
+        for f in range(2):
+            at = slice(f * points, (f + 1) * points)
+            synth_ref[at, part * coef_rows : (part + 1) * coef_rows] = jnp.where(
+                synth_column == f, wide, 0.0
+            ).astype(bf16)
+            analysis_ref[part, :, at] = jnp.where(analysis_row == f, tall, 0.0).astype(bf16)
+    forward_pass(3)
+    send_across(1)
 
     low, high = region_ref[2], region_ref[3]
     lon = lax.broadcasted_iota(jnp.int32, (1, fourier_columns), 1)
@@ -359,50 +384,41 @@
     region_weights = jnp.where((lat >= region_ref[0]) & (lat < region_ref[1]), weights, 0.0)
     weight_sum = jnp.sum(region_weights, axis=1, keepdims=True) * (high - low).astype(f32)
 
-    for t in range(STEPS + 4):
-        if t < STEPS:
-            forward_pass(t)
-            lowest_coef(t)
-        if t == STEPS - 1:
-            low_sent[...] = low_ref[...].astype(bf16)
-            low_held[pl.ds(pl.multiple_of(me * 16, 16), 16)] = low_sent[...]
-            for d in range(1, WAVES):
-                low_copy(d).start()
-        if 1 <= t <= STEPS:
-            send_across(t - 1)
-        if t >= 4:
-            take_source(t - 4)
-    held[mine] = sent[mine]
-
-    for copy in go:
-        copy.wait_recv()
-
-    coefs = held[...]
+    send_across(2)
     scaled = weights * (scale * scale)
-    for k in range(2):
-        rows = slice(k * 2 * points, (k + 1) * 2 * points)
-        grid = jnp.dot(synth_ref[0, rows], coefs, preferred_element_type=f32) + jnp.dot(
-            synth_ref[1, rows], coefs, preferred_element_type=f32
+
+    def grid_phase(h):
+        for c in range(CHUNKS):
+            for d in (2, 1, 3):
+                go_copy(h, c, d).wait_recv()
+        coefs = held[h]
+        grid = jnp.dot(
+            synth_ref[...], jnp.concatenate([coefs, coefs], axis=0), preferred_element_type=f32
         )
         wind = grid[:points]
         weighted = wind * scaled
-        flux[k * 2 * points : (k * 2 + 1) * points] = (0.5 * weighted * wind).astype(bf16)
-        flux[(k * 2 + 1) * points : (k * 2 + 2) * points] = (weighted * grid[points:]).astype(bf16)
-    fluxes = flux[...]
-    back_sent[...] = (
-        analysis_scale
-        * (
-            jnp.dot(analysis_ref[0], fluxes, preferred_element_type=f32)
-            + jnp.dot(analysis_ref[1], fluxes, preferred_element_type=f32)
-        )
-    ).astype(bf16)
-    ret = []
+        flux[h, :points] = (0.5 * weighted * wind).astype(bf16)
+        flux[h, points:] = (weighted * grid[points:]).astype(bf16)
+        fluxes = flux[h]
+        back_sent[h] = (
+            analysis_scale
+            * (
+                jnp.dot(analysis_ref[0], fluxes, preferred_element_type=f32)
+                + jnp.dot(analysis_ref[1], fluxes, preferred_element_type=f32)
+            )
+        ).astype(bf16)
+        for c in range(CHUNKS):
+            for d in (2, 1, 3):
+                ret_copy(h, c, d).start()
+        back[h, mine] = back_sent[h, mine]
+
+    grid_phase(1)
+    send_across(3)
     for c in range(CHUNKS):
-        for d in (2, 1, 3):
-            copy = wave_copy(back_sent, back, my_rows + c * PART_ROWS, c, d, ret_send, ret_recv)
-            copy.start()
-            ret.append(copy)
-    back[mine] = back_sent[mine]
+        for g in range(c * 2, c * 2 + 2):
+            chosen[g * ROWS : (g + 1) * ROWS] = take_source(g)
+        transform(0, c)
+    held[0, mine] = sent[0, mine]
 
     for d in range(1, WAVES):
         low_copy(d).wait()
@@ -419,12 +435,12 @@
     degree = lax.broadcasted_iota(jnp.int32, (1, degrees), 1).astype(f32)
     keep = 1.0 / (1.0 + ((degree + 1.0) / degrees) ** 2)
     backward = table_ref[:, columns + 384 : columns + 384 + CHUNK_ROWS]
-    for c in range(CHUNKS):
-        for copy in ret[c * (WAVES - 1) : (c + 1) * (WAVES - 1)]:
-            copy.wait_recv()
+    def tendencies(h, c):
+        for d in (2, 1, 3):
+            ret_copy(h, c, d).wait_recv()
         arrived = jnp.concatenate(
             [
-                back[w * OWNED_ROWS + c * PART_ROWS : w * OWNED_ROWS + (c + 1) * PART_ROWS]
+                back[h, w * OWNED_ROWS + c * PART_ROWS : w * OWNED_ROWS + (c + 1) * PART_ROWS]
                 for w in range(WAVES)
             ],
             axis=0,
@@ -432,26 +448,58 @@
         plain = jnp.dot(backward, arrived, preferred_element_type=f32).astype(bf16)
         for i in range(PAIR):
             m = c * PAIR + i
+            rows = slice(m * SET_ROWS, (m + 1) * SET_ROWS)
             tendency = lax.dot_general(
-                plain[i * ROWS : (i + 1) * ROWS],
+                plain[i * SET_ROWS : (i + 1) * SET_ROWS],
                 leg[m],
                 (((1,), (1,)), ((), ())),
                 preferred_element_type=f32,
             )
-            wave_id = (me * STEPS + m).astype(f32)
+            wave_id = (me * LOCAL_WAVES + m).astype(f32)
             advection = wave_id * (advect_rate / waves_total)
-            source = chosen[m * ROWS : (m + 1) * ROWS].astype(f32)
-            out_ref[m * ROWS : (m + 1) * ROWS] = (source + advection * tendency) * keep
-
-    for copy in go + ret:
-        copy.wait_send()
-    for c in range(STEPS):
+            source = set_ref[1, rows] if h == 1 else chosen[rows].astype(f32)
+            stepped = (source + advection * tendency) * keep
+            if h == 1:
+                g = STEPS + m // 2
+                pools[g][here, (m % 2) * SET_ROWS : (m % 2 + 1) * SET_ROWS] = stepped.astype(bf16)
+                if m % 2 == 1:
+                    begin_pass(g)
+            else:
+                put_rows(m, 0, stepped)
+
+    def put_rows(m, late, values):
+        for group in range(4):
+            first = m * ROWS + group * levels + late * WAVES
+            out_ref[first : first + WAVES] = values[group * WAVES : (group + 1) * WAVES]
+
+    tendencies(1, 0)
+    tendencies(1, 1)
+    forward_pass(STEPS)
+    forward_pass(STEPS + 1)
+    grid_phase(0)
+    forward_pass(STEPS + 2)
+    forward_pass(STEPS + 3)
+    for g in range(STEPS, 2 * STEPS):
+        send_across(g)
+    tendencies(0, 0)
+    tendencies(0, 1)
+    for g in range(STEPS, 2 * STEPS):
+        block = take_source(g).astype(f32)
+        for i in range(2):
+            put_rows((g - STEPS) * 2 + i, 1, block[i * SET_ROWS : (i + 1) * SET_ROWS])
+
+    for h in range(2):
+        for c in range(CHUNKS):
+            for d in (2, 1, 3):
+                go_copy(h, c, d).wait_send()
+                ret_copy(h, c, d).wait_send()
+    for c in range(2 * STEPS):
         for kind in range(3):
             pass_copy(c, kind).wait_send()
 
     @pl.when(inner)
     def _():
-        for c in range(STEPS):
+        for c in range(2 * STEPS):
             for far in range(2):
                 cross_copy(c, far).wait_send()
 
@@ -462,7 +510,7 @@
     points = quadrature_points(waves_total)
     table_high, table_low = split_table(wave_table(waves_total, points))
     fourier = wave_table(waves_total, NLON).astype(jnp.bfloat16)
-    forward, backward = order_tables(state.shape[2] // 4)
+    forward, backward = order_tables()
     unused = np.zeros((CHUNK_ROWS, 128 - CHUNK_ROWS), jnp.bfloat16)
     flat = [t.reshape(2 * waves_total, -1) for t in (fourier, table_high, table_low)]
     table = np.concatenate(flat + [forward, unused, backward, unused], axis=1)
@@ -471,7 +519,7 @@
     hbm = pl.BlockSpec(memory_space=pl.ANY)
     rows = waves_local * ROWS
     block = (rows, degrees)
-    grid_rows = (rows, latitudes)
+    grid_rows = (2, 4 * waves_total, latitudes)
     dma = pltpu.SemaphoreType.DMA
     bf16 = jnp.bfloat16
     stepped, scores = pl.pallas_call(
@@ -490,40 +538,41 @@
         out_specs=(vmem, vmem),
         scratch_shapes=[
             pltpu.VMEM(block, jnp.float32),
+            pltpu.VMEM((2, rows // 2, degrees), jnp.float32),
             pltpu.VMEM(table.shape, bf16),
-            pltpu.VMEM((2, 4 * points, 8 * waves_total), bf16),
-            pltpu.VMEM((2, 8 * waves_total, 4 * points), bf16),
+            pltpu.VMEM((2 * points, 8 * waves_total), bf16),
+            pltpu.VMEM((2, 4 * waves_total, 2 * points), bf16),
             pltpu.VMEM((2 * waves_local, latitudes), jnp.float32),
             pltpu.VMEM((2 * waves_local, latitudes), bf16),
             pltpu.VMEM((2 * waves_total, latitudes), bf16),
-            pltpu.VMEM(block, bf16),
+            pltpu.VMEM((rows // 2, degrees), bf16),
             pltpu.VMEM(legendre.shape, bf16),
             pltpu.VMEM(grid_rows, bf16),
             pltpu.VMEM(grid_rows, bf16),
-            pltpu.VMEM((4 * points, latitudes), bf16),
+            pltpu.VMEM((2, 2 * points, latitudes), bf16),
             pltpu.VMEM(grid_rows, bf16),
             pltpu.VMEM(grid_rows, bf16),
-            pltpu.VMEM((STEPS, 2, ROWS, degrees), bf16),
-            pltpu.VMEM((STEPS, ROWS, degrees), bf16),
+            pltpu.VMEM((2 * STEPS, 2, ROWS, degrees), bf16),
+            pltpu.VMEM((2 * STEPS, ROWS, degrees), bf16),
         ]
-        + [pltpu.VMEM((4, ROWS, degrees), bf16)] * STEPS
+        + [pltpu.VMEM((4, ROWS, degrees), bf16)] * (2 * STEPS)
         + [
             dma((CHUNKS,)),
             dma,
-            dma((STEPS,)),
-            dma((WAVES - 1, CHUNKS)),
-            dma((WAVES - 1, CHUNKS)),
-            dma((WAVES - 1, CHUNKS)),
-            dma((WAVES - 1, CHUNKS)),
+            dma((LOCAL_WAVES,)),
+            dma((2, WAVES - 1, CHUNKS)),
+            dma((2, WAVES - 1, CHUNKS)),
+            dma((2, WAVES - 1, CHUNKS)),
+            dma((2, WAVES - 1, CHUNKS)),
             dma((WAVES - 1,)),
             dma((WAVES - 1,)),
-            dma((3, STEPS)),
-            dma((3, STEPS)),
-            dma((2, STEPS)),
-            dma((STEPS,)),
+            dma((3, 2 * STEPS)),
+            dma((3, 2 * STEPS)),
+            dma((2, 2 * STEPS)),
+            dma((2 * STEPS,)),
         ],
         compiler_params=pltpu.CompilerParams(
-            collective_id=0, has_side_effects=True, vmem_limit_bytes=48 * 1024 * 1024
+            collective_id=0, has_side_effects=True, vmem_limit_bytes=56 * 1024 * 1024
         ),
     )(state.reshape(block), legendre, lat_weights, region, sources, jnp.asarray(table))
     return (stepped.reshape(state.shape), scores[0, :1])

time: 47 us -> 40.7 us (0.87)
  Pallas kernels: 40.7 us -> 36.7 us
  local copies, waits for them, and re-layouts: 5.42 us -> 3.16 us
    pallas_call x1, Pallas kernels: 40.7 us -> 36.7 us  [in_one_kernel(): pl.pallas_call(functools.partial(step_kernel, scale=(2.0 * waves_total) *...]
    unnamed x11 -> x1, local copies, waits for them, and re-layouts: 4.91 us -> 1.97 us
    slice x1, local copies, waits for them, and re-layouts: 0.51 us -> 1.19 us  [in_one_kernel(): return (stepped.reshape(state.shape), scores[0, :1])]
where the time goes in v5:
time: 40.7 us; the launch traced here: 40.5 us
  Pallas kernels  36.7 us (90%)
  local copies, waits for them, and re-layouts  3.16 us (8%)
  between operations  0.64 us (2%)
    pallas_call x1, Pallas kernels, in_one_kernel(): pl.pallas_call(functools.partial(step_kernel, scale=(2.0 * waves_total) *...  36.7 us
    unnamed x1, local copies, waits for them, and re-layouts  1.97 us
    slice x1, local copies, waits for them, and re-layouts, in_one_kernel(): return (stepped.reshape(state.shape), scores[0, :1])  1.19 us

profile of v5, /device:TPU:0, one launch (start us, length us, event | category | flops | bytes accessed | tf_op | source)
XLA Modules:
  0.0 40.5 jit_solution(2711242160594411986)
XLA Ops:
  0.6 36.7 %shard_map.77 = (f32[256,640]{1,0:T(8,128)}, f32[8,128]{1,0:T(8,128)}) custom-call(f32[256,640]{1,0:T(8,128)} %bitcast.3, bf16[8,640,640]{2,1,0:T(8,128)(2,1)} %legendre_ref.1, f32[640]{0:T(1024)} %weights_ref.1, s32[4]{0:T(128)} %region_ref.1, s32[8]{0:T(128)} %sources_ref.1, bf16[64,3072]{1,0:T(8,128)(2,1)} %constant.2.clone.table_hbm), custom_call_target="tpu_custom_call" | custom-call | tf_op jit(solution)/shard_map/pallas_call | solution.py:525
  37.3 1.2 %slice.3 = f32[1,1]{1,0:T(1,128)} slice(f32[8,128]{1,0:T(8,128)} %get-tuple-element.5), slice={[0:1], [0:1]} | slice | bytes 8 | tf_op jit(solution)/shard_map/slice | solution.py:578
  38.5 2.0 %copy.9 = f32[1,8,32,640]{3,2,1,0:T(8,128)} copy(f32[1,8,32,640]{3,2,1,0:T(8,128)} %bitcast.4) | data formatting | bytes 1310720

commit v6 on v5

--- a/solution.py
+++ b/solution.py
@@ -414,11 +414,13 @@
 
     grid_phase(1)
     send_across(3)
-    for c in range(CHUNKS):
+
+    def transform_sources(c):
         for g in range(c * 2, c * 2 + 2):
             chosen[g * ROWS : (g + 1) * ROWS] = take_source(g)
         transform(0, c)
-    held[0, mine] = sent[0, mine]
+
+    transform_sources(0)
 
     for d in range(1, WAVES):
         low_copy(d).wait()
@@ -472,21 +474,30 @@
             first = m * ROWS + group * levels + late * WAVES
             out_ref[first : first + WAVES] = values[group * WAVES : (group + 1) * WAVES]
 
+    def put_cloned(g):
+        block = take_source(g).astype(f32)
+        for i in range(2):
+            put_rows((g - STEPS) * 2 + i, 1, block[i * SET_ROWS : (i + 1) * SET_ROWS])
+
     tendencies(1, 0)
     tendencies(1, 1)
     forward_pass(STEPS)
     forward_pass(STEPS + 1)
-    grid_phase(0)
+    transform_sources(1)
+    held[0, mine] = sent[0, mine]
     forward_pass(STEPS + 2)
     forward_pass(STEPS + 3)
-    for g in range(STEPS, 2 * STEPS):
-        send_across(g)
+    send_across(STEPS)
+    send_across(STEPS + 1)
+    grid_phase(0)
+    send_across(STEPS + 2)
+    send_across(STEPS + 3)
     tendencies(0, 0)
+    put_cloned(STEPS)
+    put_cloned(STEPS + 1)
     tendencies(0, 1)
-    for g in range(STEPS, 2 * STEPS):
-        block = take_source(g).astype(f32)
-        for i in range(2):
-            put_rows((g - STEPS) * 2 + i, 1, block[i * SET_ROWS : (i + 1) * SET_ROWS])
+    put_cloned(STEPS + 2)
+    put_cloned(STEPS + 3)
 
     for h in range(2):
         for c in range(CHUNKS):

time: 40.7 us -> 40.9 us (level)
  no operation moved by 1% of the time
where the time goes in v6:
time: 40.9 us; the launch traced here: 40.7 us
  Pallas kernels  36.9 us (90%)
  local copies, waits for them, and re-layouts  3.16 us (8%)
  between operations  0.64 us (2%)
    pallas_call x1, Pallas kernels, in_one_kernel(): pl.pallas_call(functools.partial(step_kernel, scale=(2.0 * waves_total) *...  36.9 us
    unnamed x1, local copies, waits for them, and re-layouts  1.97 us
    slice x1, local copies, waits for them, and re-layouts, in_one_kernel(): return (stepped.reshape(state.shape), scores[0, :1])  1.19 us

profile of v6, /device:TPU:0, one launch (start us, length us, event | category | flops | bytes accessed | tf_op | source)
XLA Modules:
  0.0 40.7 jit_solution(10950287879481024057)
XLA Ops:
  0.6 36.9 %shard_map.77 = (f32[256,640]{1,0:T(8,128)}, f32[8,128]{1,0:T(8,128)}) custom-call(f32[256,640]{1,0:T(8,128)} %bitcast.3, bf16[8,640,640]{2,1,0:T(8,128)(2,1)} %legendre_ref.1, f32[640]{0:T(1024)} %weights_ref.1, s32[4]{0:T(128)} %region_ref.1, s32[8]{0:T(128)} %sources_ref.1, bf16[64,3072]{1,0:T(8,128)(2,1)} %constant.2.clone.table_hbm), custom_call_target="tpu_custom_call" | custom-call | tf_op jit(solution)/shard_map/pallas_call | solution.py:536
  37.5 1.2 %slice.3 = f32[1,1]{1,0:T(1,128)} slice(f32[8,128]{1,0:T(8,128)} %get-tuple-element.5), slice={[0:1], [0:1]} | slice | bytes 8 | tf_op jit(solution)/shard_map/slice | solution.py:589
  38.7 2.0 %copy.9 = f32[1,8,32,640]{3,2,1,0:T(8,128)} copy(f32[1,8,32,640]{3,2,1,0:T(8,128)} %bitcast.4) | data formatting | bytes 1310720

commit v7 on v6

--- a/solution.py
+++ b/solution.py
@@ -437,6 +437,8 @@
     degree = lax.broadcasted_iota(jnp.int32, (1, degrees), 1).astype(f32)
     keep = 1.0 / (1.0 + ((degree + 1.0) / degrees) ** 2)
     backward = table_ref[:, columns + 384 : columns + 384 + CHUNK_ROWS]
+    lane_wave = lax.broadcasted_iota(jnp.int32, (degrees, 2 * CHUNK_ROWS), 1) % CHUNK_ROWS // SET_ROWS
+
     def tendencies(h, c):
         for d in (2, 1, 3):
             ret_copy(h, c, d).wait_recv()
@@ -448,15 +450,20 @@
             axis=0,
         )
         plain = jnp.dot(backward, arrived, preferred_element_type=f32).astype(bf16)
+        twice = jnp.concatenate([plain, plain], axis=0)
+        for i in range(PAIR):
+            product = lax.dot_general(
+                leg[c * PAIR + i],
+                twice,
+                (((1,), (1,)), ((), ())),
+                preferred_element_type=f32,
+            )
+            columns_of = product if i == 0 else jnp.where(lane_wave == i, product, columns_of)
+        turned = columns_of.T
         for i in range(PAIR):
             m = c * PAIR + i
             rows = slice(m * SET_ROWS, (m + 1) * SET_ROWS)
-            tendency = lax.dot_general(
-                plain[i * SET_ROWS : (i + 1) * SET_ROWS],
-                leg[m],
-                (((1,), (1,)), ((), ())),
-                preferred_element_type=f32,
-            )
+            tendency = turned[i * SET_ROWS : (i + 1) * SET_ROWS]
             wave_id = (me * LOCAL_WAVES + m).astype(f32)
             advection = wave_id * (advect_rate / waves_total)
             source = set_ref[1, rows] if h == 1 else chosen[rows].astype(f32)

time: 40.9 us -> 41.4 us (1.012)
  Pallas kernels: 36.9 us -> 37.4 us
    pallas_call x1, Pallas kernels: 36.9 us -> 37.4 us  [in_one_kernel(): pl.pallas_call(functools.partial(step_kernel, scale=(2.0 * waves_total) *...]
where the time goes in v7:
time: 41.4 us; the launch traced here: 41.2 us
  Pallas kernels  37.4 us (90%)
  local copies, waits for them, and re-layouts  3.16 us (8%)
  between operations  0.64 us (2%)
    pallas_call x1, Pallas kernels, in_one_kernel(): pl.pallas_call(functools.partial(step_kernel, scale=(2.0 * waves_total) *...  37.4 us
    unnamed x1, local copies, waits for them, and re-layouts  1.97 us
    slice x1, local copies, waits for them, and re-layouts, in_one_kernel(): return (stepped.reshape(state.shape), scores[0, :1])  1.19 us

profile of v7, /device:TPU:0, one launch (start us, length us, event | category | flops | bytes accessed | tf_op | source)
XLA Modules:
  0.0 41.2 jit_solution(2263798980006963837)
XLA Ops:
  0.6 37.4 %shard_map.77 = (f32[256,640]{1,0:T(8,128)}, f32[8,128]{1,0:T(8,128)}) custom-call(f32[256,640]{1,0:T(8,128)} %bitcast.3, bf16[8,640,640]{2,1,0:T(8,128)(2,1)} %legendre_ref.1, f32[640]{0:T(1024)} %weights_ref.1, s32[4]{0:T(128)} %region_ref.1, s32[8]{0:T(128)} %sources_ref.1, bf16[64,3072]{1,0:T(8,128)(2,1)} %constant.2.clone.table_hbm), custom_call_target="tpu_custom_call" | custom-call | tf_op jit(solution)/shard_map/pallas_call | solution.py:543
  38.0 1.2 %slice.3 = f32[1,1]{1,0:T(1,128)} slice(f32[8,128]{1,0:T(8,128)} %get-tuple-element.5), slice={[0:1], [0:1]} | slice | bytes 8 | tf_op jit(solution)/shard_map/slice | solution.py:596
  39.2 2.0 %copy.9 = f32[1,8,32,640]{3,2,1,0:T(8,128)} copy(f32[1,8,32,640]{3,2,1,0:T(8,128)} %bitcast.4) | data formatting | bytes 1310720

commit v8 on v6

--- a/solution.py
+++ b/solution.py
@@ -208,6 +208,46 @@
         for g in range(c * 2, c * 2 + 2):
             pools[g][here] = set_ref[0, g * ROWS : (g + 1) * ROWS].astype(bf16)
 
+    columns = fourier_columns = table_ref.shape[1] - 4 * 128
+    table_load.wait()
+    coef_rows = 4 * waves_total
+    owner_of = lax.broadcasted_iota(jnp.int32, (2 * waves_total, coef_rows), 0)
+    column = lax.broadcasted_iota(jnp.int32, (2 * waves_total, coef_rows), 1)
+    widen = jnp.where(column // 2 == owner_of, 1.0, 0.0).astype(bf16)
+    tall_owner = lax.broadcasted_iota(jnp.int32, (coef_rows, 2 * waves_total), 1)
+    tall_row = lax.broadcasted_iota(jnp.int32, (coef_rows, 2 * waves_total), 0)
+    lengthen = jnp.where(tall_row // 2 == tall_owner, 1.0, 0.0).astype(bf16)
+    synth_column = lax.broadcasted_iota(jnp.int32, (points, coef_rows), 1) % 2
+    analysis_row = lax.broadcasted_iota(jnp.int32, (coef_rows, points), 0) % 2
+    for part in range(2):
+        waves = table_ref[:, columns + part * 128 : columns + part * 128 + points]
+        wide = lax.dot_general(
+            waves, widen, (((0,), (0,)), ((), ())), preferred_element_type=f32
+        )
+        tall = jnp.dot(lengthen, waves, preferred_element_type=f32)
+        for f in range(2):
+            at = slice(f * points, (f + 1) * points)
+            synth_ref[at, part * coef_rows : (part + 1) * coef_rows] = jnp.where(
+                synth_column == f, wide, 0.0
+            ).astype(bf16)
+            analysis_ref[part, :, at] = jnp.where(analysis_row == f, tall, 0.0).astype(bf16)
+    low, high = region_ref[2], region_ref[3]
+    lon = lax.broadcasted_iota(jnp.int32, (1, fourier_columns), 1)
+    lon_inside = jnp.where((lon >= low) & (lon < high), 1.0, 0.0)
+    fourier = table_ref[:, :fourier_columns]
+    gram = lax.dot_general(
+        (fourier.astype(f32) * lon_inside).astype(bf16),
+        fourier,
+        (((1,), (1,)), ((), ())),
+        preferred_element_type=f32,
+    )
+    gram_high = gram.astype(bf16)
+    gram_low = (gram - gram_high.astype(f32)).astype(bf16)
+    lat = lax.broadcasted_iota(jnp.int32, (1, lat_count), 1)
+    weights = weights_ref[...].reshape(1, lat_count)
+    region_weights = jnp.where((lat >= region_ref[0]) & (lat < region_ref[1]), weights, 0.0)
+    weight_sum = jnp.sum(region_weights, axis=1, keepdims=True) * (high - low).astype(f32)
+
     @pl.when(inner)
     def _():
         pl.semaphore_wait(barrier, 7)
@@ -294,7 +334,6 @@
 
     my_rows = me * OWNED_ROWS
     mine = pl.ds(pl.multiple_of(my_rows, OWNED_ROWS), OWNED_ROWS)
-    columns = fourier_columns = table_ref.shape[1] - 4 * 128
 
     def go_copy(h, c, d):
         return wave_copy(sent, held, h, c, d, go_send, go_recv)
@@ -330,7 +369,6 @@
         cross_copy(g, 0).wait_recv()
         return jnp.where(near, pools[g][choice], crossed[g])
 
-    table_load.wait()
     transform(1, 0)
     forward_pass(0)
     transform(1, 1)
@@ -343,47 +381,8 @@
     forward_pass(2)
     send_across(0)
 
-    coef_rows = 4 * waves_total
-    owner_of = lax.broadcasted_iota(jnp.int32, (2 * waves_total, coef_rows), 0)
-    column = lax.broadcasted_iota(jnp.int32, (2 * waves_total, coef_rows), 1)
-    widen = jnp.where(column // 2 == owner_of, 1.0, 0.0).astype(bf16)
-    tall_owner = lax.broadcasted_iota(jnp.int32, (coef_rows, 2 * waves_total), 1)
-    tall_row = lax.broadcasted_iota(jnp.int32, (coef_rows, 2 * waves_total), 0)
-    lengthen = jnp.where(tall_row // 2 == tall_owner, 1.0, 0.0).astype(bf16)
-    synth_column = lax.broadcasted_iota(jnp.int32, (points, coef_rows), 1) % 2
-    analysis_row = lax.broadcasted_iota(jnp.int32, (coef_rows, points), 0) % 2
-    for part in range(2):
-        waves = table_ref[:, columns + part * 128 : columns + part * 128 + points]
-        wide = lax.dot_general(
-            waves, widen, (((0,), (0,)), ((), ())), preferred_element_type=f32
-        )
-        tall = jnp.dot(lengthen, waves, preferred_element_type=f32)
-        for f in range(2):
-            at = slice(f * points, (f + 1) * points)
-            synth_ref[at, part * coef_rows : (part + 1) * coef_rows] = jnp.where(
-                synth_column == f, wide, 0.0
-            ).astype(bf16)
-            analysis_ref[part, :, at] = jnp.where(analysis_row == f, tall, 0.0).astype(bf16)
     forward_pass(3)
     send_across(1)
-
-    low, high = region_ref[2], region_ref[3]
-    lon = lax.broadcasted_iota(jnp.int32, (1, fourier_columns), 1)
-    lon_inside = jnp.where((lon >= low) & (lon < high), 1.0, 0.0)
-    fourier = table_ref[:, :fourier_columns]
-    gram = lax.dot_general(
-        (fourier.astype(f32) * lon_inside).astype(bf16),
-        fourier,
-        (((1,), (1,)), ((), ())),
-        preferred_element_type=f32,
-    )
-    gram_high = gram.astype(bf16)
-    gram_low = (gram - gram_high.astype(f32)).astype(bf16)
-    lat = lax.broadcasted_iota(jnp.int32, (1, lat_count), 1)
-    weights = weights_ref[...].reshape(1, lat_count)
-    region_weights = jnp.where((lat >= region_ref[0]) & (lat < region_ref[1]), weights, 0.0)
-    weight_sum = jnp.sum(region_weights, axis=1, keepdims=True) * (high - low).astype(f32)
-
     send_across(2)
     scaled = weights * (scale * scale)
 

time: 40.9 us -> 41.3 us (level)
    pallas_call x1, Pallas kernels: 36.9 us -> 37.3 us  [in_one_kernel(): pl.pallas_call(functools.partial(step_kernel, scale=(2.0 * waves_total) *...]
where the time goes in v8:
time: 41.3 us; the launch traced here: 41.1 us
  Pallas kernels  37.3 us (90%)
  local copies, waits for them, and re-layouts  3.16 us (8%)
  between operations  0.64 us (2%)
    pallas_call x1, Pallas kernels, in_one_kernel(): pl.pallas_call(functools.partial(step_kernel, scale=(2.0 * waves_total) *...  37.3 us
    unnamed x1, local copies, waits for them, and re-layouts  1.97 us
    slice x1, local copies, waits for them, and re-layouts, in_one_kernel(): return (stepped.reshape(state.shape), scores[0, :1])  1.19 us

profile of v8, /device:TPU:0, one launch (start us, length us, event | category | flops | bytes accessed | tf_op | source)
XLA Modules:
  0.0 41.1 jit_solution(12340292251206017520)
XLA Ops:
  0.6 37.3 %shard_map.77 = (f32[256,640]{1,0:T(8,128)}, f32[8,128]{1,0:T(8,128)}) custom-call(f32[256,640]{1,0:T(8,128)} %bitcast.3, bf16[8,640,640]{2,1,0:T(8,128)(2,1)} %legendre_ref.1, f32[640]{0:T(1024)} %weights_ref.1, s32[4]{0:T(128)} %region_ref.1, s32[8]{0:T(128)} %sources_ref.1, bf16[64,3072]{1,0:T(8,128)(2,1)} %constant.2.clone.table_hbm), custom_call_target="tpu_custom_call" | custom-call | tf_op jit(solution)/shard_map/pallas_call | solution.py:535
  37.9 1.2 %slice.3 = f32[1,1]{1,0:T(1,128)} slice(f32[8,128]{1,0:T(8,128)} %get-tuple-element.5), slice={[0:1], [0:1]} | slice | bytes 8 | tf_op jit(solution)/shard_map/slice | solution.py:588
  39.1 2.0 %copy.9 = f32[1,8,32,640]{3,2,1,0:T(8,128)} copy(f32[1,8,32,640]{3,2,1,0:T(8,128)} %bitcast.4) | data formatting | bytes 1310720

commit v9 on v6

--- a/solution.py
+++ b/solution.py
@@ -432,7 +432,7 @@
         region_weights * (scale * scale)
     )
     score = jnp.sum(squares, axis=1, keepdims=True) / weight_sum
-    score_ref[...] = jnp.broadcast_to(score, score_ref.shape)
+    score_ref[0] = jnp.sum(score)
 
     degree = lax.broadcasted_iota(jnp.int32, (1, degrees), 1).astype(f32)
     keep = 1.0 / (1.0 + ((degree + 1.0) / degrees) ** 2)
@@ -543,10 +543,10 @@
         ),
         out_shape=(
             jax.ShapeDtypeStruct(block, jnp.float32),
-            jax.ShapeDtypeStruct((8, 128), jnp.float32),
+            jax.ShapeDtypeStruct((1,), jnp.float32),
         ),
         in_specs=[hbm, hbm, vmem, smem, smem, hbm],
-        out_specs=(vmem, vmem),
+        out_specs=(vmem, smem),
         scratch_shapes=[
             pltpu.VMEM(block, jnp.float32),
             pltpu.VMEM((2, rows // 2, degrees), jnp.float32),
@@ -586,7 +586,7 @@
             collective_id=0, has_side_effects=True, vmem_limit_bytes=56 * 1024 * 1024
         ),
     )(state.reshape(block), legendre, lat_weights, region, sources, jnp.asarray(table))
-    return (stepped.reshape(state.shape), scores[0, :1])
+    return (stepped.reshape(state.shape), scores)
 
 
 def solution(mesh):

time: 40.9 us -> 41.5 us (1.015)
  between operations: 0.64 us -> 2.39 us
  local copies, waits for them, and re-layouts: 3.16 us -> 1.97 us
    slice x1 -> x0, local copies, waits for them, and re-layouts: 1.19 us -> none  [in_one_kernel(): return (stepped.reshape(state.shape), scores[0, :1])]
where the time goes in v9:
time: 41.5 us; the launch traced here: 41.3 us
  Pallas kernels  36.9 us (89%)
  between operations  2.39 us (6%)
  local copies, waits for them, and re-layouts  1.97 us (5%)
    pallas_call x1, Pallas kernels, in_one_kernel(): pl.pallas_call(functools.partial(step_kernel, scale=(2.0 * waves_total) *...  36.9 us
    unnamed x1, local copies, waits for them, and re-layouts  1.97 us

profile of v9, /device:TPU:0, one launch (start us, length us, event | category | flops | bytes accessed | tf_op | source)
XLA Modules:
  0.0 41.3 jit_solution(13513833692369948550)
XLA Ops:
  0.6 36.9 %shard_map.77 = (f32[256,640]{1,0:T(8,128)}, f32[1]{0:T(128)}) custom-call(f32[256,640]{1,0:T(8,128)} %bitcast.2, bf16[8,640,640]{2,1,0:T(8,128)(2,1)} %legendre_ref.1, f32[640]{0:T(1024)} %weights_ref.1, s32[4]{0:T(128)} %region_ref.1, s32[8]{0:T(128)} %sources_ref.1, bf16[64,3072]{1,0:T(8,128)(2,1)} %constant.2.clone.table_hbm), custom_call_target="tpu_custom_call" | custom-call | tf_op jit(solution)/shard_map/pallas_call | solution.py:536
  37.6 2.0 %copy.10 = f32[1,8,32,640]{3,2,1,0:T(8,128)} copy(f32[1,8,32,640]{3,2,1,0:T(8,128)} %bitcast.3) | data formatting | bytes 1310720
